TPU v7x, 32 devices: a whole 2x2x4 slice. The times are simulated.
32 devices in a mesh: grp: 4 (over z), dev: 8 (over y, x, core).
Axes of the slice: x: 2, y: 2, z: 4, core: 2. Of those that a mesh axis runs over, the one named last changes fastest.
Arguments:
- orbitals: bfloat16 [4, 8, 64, 2, 2304], P('grp', 'dev'), may hold values from -6 to 6
- potential: bfloat16 [8, 2304], P('dev'), may hold values from -4 to 4
- counts: int32 [4, 8], P('grp'), may hold values from 16 to 64, as said below
- parity: int32 [4, 8], P('grp', 'dev'), may hold values 0 or 1
Outputs:
- density: float32 [8, 1, 2304], P('dev', None, 'grp')
- filtered: bfloat16 [4, 8, 64, 2, 2304], P('grp', 'dev')
Inputs may be any that keep to these rules, and one draw needn't show every extreme that they name: In each row of 8 fragments the counts sum to 224, and some fragment of every row holds 64 orbitals and some holds 16.
All inputs are finite; a program needn't handle non-finite values. No bound on the sum of `parity` on one device may be relied on, other than what follows from the above.
Results may differ from a plain program's by a relative error of at most 0.0026.
Values may be sent and summed in bfloat16 or wider, within the bound.
No kernel may reach another device: no remote copies, remote signals or barrier semaphores. Data moves between devices by JAX's collectives and lax.ppermute only.
A program may use at most 64 MiB of HBM per device.

v0:
```python
import jax
import jax.numpy as jnp
from jax import lax
from jax.sharding import PartitionSpec as P

MAXORB = 64
KEEP = 4
DEGREE = 8
BZ = 48
MEANORB = 28


filter_centre = 9.0
filter_half = 7.0


def from_behind(block, axis, distance):
    devices = range(lax.axis_size(axis))
    route = [((i - distance) % len(devices), i) for i in devices]
    return lax.ppermute(block, axis, route)


def beside_sum(field):
    edge_x = jnp.zeros_like(field[:, :1])
    along_x = jnp.concatenate([field[:, 1:], edge_x], 1) + jnp.concatenate(
        [edge_x, field[:, :-1]], 1
    )
    edge_y = jnp.zeros_like(field[:, :, :BZ])
    along_y = jnp.concatenate([field[:, :, BZ:], edge_y], 2) + jnp.concatenate(
        [edge_y, field[:, :, :-BZ]], 2
    )
    edge_z = jnp.zeros_like(field[:, :, :1])
    upper = jnp.concatenate([field[:, :, 1:], edge_z], 2)
    lower = jnp.concatenate([edge_z, field[:, :, :-1]], 2)
    z_index = jnp.arange(field.shape[2]) % BZ
    along_z = jnp.where(z_index == BZ - 1, 0.0, upper) + jnp.where(z_index == 0, 0.0, lower)
    return along_x + along_y + along_z


def step_map(field, patches):
    return (6.0 * field - beside_sum(field) + patches * field - filter_centre * field) / filter_half


def chebyshev_rows(orbital_rows, patches):
    previous = orbital_rows.astype(jnp.float32)
    current = step_map(previous, patches)
    for degree_step in range(DEGREE - 1):
        previous, current = (current, 2.0 * step_map(current, patches) - previous)
    mean_square = jnp.mean(current * current, axis=(1, 2), keepdims=True)
    return (current * lax.rsqrt(mean_square + 1e-06)).astype(jnp.bfloat16)


def on_device(orbitals, potential, counts, parity):
    group_size = lax.axis_size("dev")
    my_index = lax.axis_index("dev")
    orbital_rows = orbitals[0, 0]
    box_shape = orbital_rows.shape[1:]
    blocks_x = potential.shape[0]
    plane_cells = potential.shape[1]
    received = MEANORB - KEEP
    capacity = (MAXORB - KEEP + group_size - 1) // group_size
    bf_zero = jnp.zeros((), jnp.bfloat16)
    full_line = lax.all_gather(potential, "dev", axis=0, tiled=True)
    looped = jnp.concatenate([full_line, full_line[:blocks_x]], 0)
    own_patch = lax.dynamic_slice_in_dim(looped, my_index * blocks_x, 2 * blocks_x, 0)
    counts_row = counts[0]
    excess = counts_row - KEEP
    excess_ends = jnp.cumsum(excess)
    starts = excess_ends - excess
    device_ids = jnp.arange(group_size, dtype=jnp.int32)
    my_start = jnp.sum(jnp.where(device_ids == my_index, starts, 0))
    my_excess = jnp.sum(jnp.where(device_ids == my_index, excess, 0))
    my_count = my_excess + KEEP
    slot_ids = jnp.arange(capacity, dtype=jnp.int32)
    offset = jnp.mod(device_ids[:, None] - my_start, group_size) + slot_ids[None, :] * group_size
    is_live = offset < my_excess
    source = jnp.where(is_live, KEEP + offset, 0).reshape(-1)
    picked = jnp.take(orbital_rows, source, axis=0).reshape((group_size, capacity) + box_shape)
    outgoing = jnp.where(is_live[:, :, None, None], picked, bf_zero)
    turn_ids = jnp.arange(received, dtype=jnp.int32)
    global_ids = my_index + turn_ids * group_size
    sender = jnp.sum((excess_ends[None, :] <= global_ids[:, None]).astype(jnp.int32), axis=1)
    sender_start = jnp.sum(
        jnp.where(device_ids[None, :] == sender[:, None], starts[None, :], 0), axis=1
    )
    flat_ids = sender * capacity + (global_ids - sender_start) // group_size
    incoming = lax.all_to_all(outgoing, "dev", split_axis=0, concat_axis=0, tiled=True)
    taken = jnp.take(incoming.reshape((group_size * capacity,) + box_shape), flat_ids, axis=0)
    plane_ids = (
        sender[:, None] * blocks_x + jnp.arange(2 * blocks_x, dtype=jnp.int32)[None, :]
    ) % (group_size * blocks_x)
    far_patch = jnp.take(full_line, plane_ids.reshape(-1), axis=0).reshape((received,) + box_shape)
    work_rows = jnp.concatenate([orbital_rows[:KEEP], taken], 0)
    patch_rows = jnp.concatenate(
        [jnp.broadcast_to(own_patch, (KEEP,) + box_shape), far_patch], 0
    ).astype(jnp.float32)
    filtered_work = chebyshev_rows(work_rows, patch_rows)
    back_offset = jnp.mod(my_index - starts[:, None], group_size) + slot_ids[None, :] * group_size
    back_live = back_offset < excess[:, None]
    back_rows = jnp.where(
        back_live, KEEP + (starts[:, None] + back_offset - my_index) // group_size, 0
    )
    back_picked = jnp.take(filtered_work, back_rows.reshape(-1), axis=0).reshape(
        (group_size, capacity) + box_shape
    )
    send_back = jnp.where(back_live[:, :, None, None], back_picked, bf_zero)
    returned = lax.all_to_all(send_back, "dev", split_axis=0, concat_axis=0, tiled=True)
    orbital_ids = jnp.arange(MAXORB, dtype=jnp.int32)
    moved = orbital_ids - KEEP
    helper = jnp.mod(my_start + moved, group_size)
    pooled = jnp.concatenate(
        [filtered_work[:KEEP], returned.reshape((group_size * capacity,) + box_shape)], 0
    )
    pool_ids = jnp.where(
        orbital_ids < KEEP,
        orbital_ids,
        KEEP + helper * capacity + jnp.maximum(moved, 0) // group_size,
    )
    restored = jnp.take(pooled, pool_ids, axis=0)
    restored = jnp.where((orbital_ids < my_count)[:, None, None], restored, bf_zero)
    squares = restored.astype(jnp.float32)
    density_part = jnp.sum(squares * squares, axis=0) * (
        (1.0 - 2.0 * parity[0, 0].astype(jnp.float32)) / MAXORB
    )
    halves = density_part.reshape(2, blocks_x, plane_cells)
    carried = from_behind(halves[1], "dev", 1)
    density = lax.psum_scatter(halves[0] + carried, "grp", scatter_dimension=1, tiled=True)
    return (density[None], restored[None, None])


def solution(mesh):
    placed = (P("grp", "dev", None, None, None), P("dev", None), P("grp", None), P("grp", "dev"))
    return jax.shard_map(
        on_device,
        mesh=mesh,
        in_specs=placed,
        out_specs=(P("dev", None, "grp"), P("grp", "dev", None, None, None)),
        check_vma=False,
    )
```

profile of v0, /device:TPU:0, one launch (start us, length us, event | category | flops | bytes accessed | tf_op | source)
XLA Modules:
  0.0 134.7 jit_solution(10558103823052373324)
XLA Ops:
  7.2 0.7 fusion.62
  8.0 0.7 fusion.60
  8.7 1.3 fusion.44
  12.0 2.8 %gather_fusion = bf16[64,2,2304]{2,1,0:T(2,128)(2,1)S(1)} fusion(bf16[64,2,2304]{2,1,0:T(2,128)(2,1)} %bitcast.64, s32[1024]{0:T(1024)S(1)} %pad_clamp_fusion.4), kind=kCustom, calls=%fused_computation | custom fusion | bytes 1179904 | tf_op jit(solution)/shard_map/jit(_take)/gather | solution.py:78
  14.8 1.6 %broadcast_select_fusion.7 = bf16[8,8,2,2304]{3,2,1,0:T(2,128)(2,1)} fusion(pred[8,8]{1,0:T(8,128)(4,1)S(1)} %get-tuple-element.59, bf16[8,8,2,2304]{3,2,1,0:T(2,128)(2,1)S(1)} %bitcast.62, pred[8,8]{1,0:T(8,128)(4,1)S(1)} %get-tuple-element.58), kind=kLoop, calls=%fused_computation.21 | loop fusion | flops 589824 | bytes 1179776 | tf_op jit(solution)/shard_map/jit(_where)/select_n | solution.py:79
  16.4 5.2 %all-to-all-start = ((bf16[8,8,2,2304]{3,2,1,0:T(2,128)(2,1)}), bf16[8,8,2,2304]{3,2,1,0:T(2,128)(2,1)S(1)}, u32[]{:S(2)}, u32[]{:S(2)}) async-start(bf16[8,8,2,2304]{3,2,1,0:T(2,128)(2,1)} %broadcast_select_fusion.7), calls=%async_computation | async-start | bytes 1179648 | tf_op jit(solution)/shard_map/all_to_all | solution.py:87
  22.0 13.5 %all-gather = bf16[8,1,2304]{2,1,0:T(2,128)(2,1)S(1)} all-gather(bf16[1,1,2304]{2,1,0:T(2,128)(2,1)S(1)} %bitcast.66), channel_id=1, replica_groups=mesh['grp'=4,'dev'=8] {'dev'}, dimensions={0}, use_global_device_ids=true | all-gather | bytes 41472 | tf_op jit(solution)/shard_map/all_gather | solution.py:63
  35.7 0.7 gather_fusion.2
  37.0 0.8 slice_bitcast_fusion
  37.8 1.0 gather_fusion.1
  41.0 2.4 %broadcast_multiply_fusion = (f32[28,2,2304]{2,1,0:T(2,128)S(1)}, f32[28,2,2304]{2,1,0:T(2,128)S(1)}) fusion(bf16[24,2,2304]{2,1,0:T(2,128)(2,1)S(1)} %broadcast_select_fusion.9, bf16[4,2,2304]{2,1,0:T(2,128)(2,1)S(1)} %broadcast_in_dim.216, f32[28,2,2303]{2,1,0:T(2,128)S(1)} %get-tuple-element.57, pred[2304]{0:T(1024)(128)(4,1)S(1)} %get-tuple-element.69, ...), kind=kLoop, calls=%fused_computation.59 | loop fusion | flops 2322432 | bytes 4111424 | tf_op jit(solution)/shard_map/div | solution.py:41
  45.0 2.4 %fusion.5 = f32[28,2,2304]{2,1,0:T(2,128)S(1)} fusion(f32[28,2,2304]{2,1,0:T(2,128)S(1)} %get-tuple-element.7, f32[28,2,2303]{2,1,0:T(2,128)S(1)} %get-tuple-element.51, f32[28,2,2303]{2,1,0:T(2,128)S(1)} %get-tuple-element.50, f32[28,2,2256]{2,1,0:T(2,128)S(1)} %get-tuple-element.49, f32[28,2,2256]{2,1,0:T(2,128)S(1)} %get-tuple-element.48, ...), kind=kLoop, calls=%fused_computation.28 | loop fusion | flops 2580480 | bytes 4111424 | tf_op jit(solution)/shard_map/sub | solution.py:48
  49.0 2.2 %fusion.9 = f32[28,2,2304]{2,1,0:T(2,128)S(1)} fusion(f32[28,2,2304]{2,1,0:T(2,128)S(1)} %fusion.5, f32[28,2,2303]{2,1,0:T(2,128)S(1)} %get-tuple-element.45, f32[28,2,2303]{2,1,0:T(2,128)S(1)} %get-tuple-element.44, f32[28,2,2256]{2,1,0:T(2,128)S(1)} %get-tuple-element.43, f32[28,2,2256]{2,1,0:T(2,128)S(1)} %get-tuple-element.42, ...), kind=kLoop, calls=%fused_computation.32 | loop fusion | flops 2322432 | bytes 4369472 | tf_op jit(solution)/shard_map/sub | solution.py:48
  52.8 2.1 %fusion.13 = f32[28,2,2304]{2,1,0:T(2,128)S(1)} fusion(f32[28,2,2304]{2,1,0:T(2,128)S(1)} %fusion.5, f32[28,2,2304]{2,1,0:T(2,128)S(1)} %fusion.9, f32[28,2,2303]{2,1,0:T(2,128)S(1)} %get-tuple-element.39, f32[28,2,2303]{2,1,0:T(2,128)S(1)} %get-tuple-element.38, f32[28,2,2256]{2,1,0:T(2,128)S(1)} %get-tuple-element.37, ...), kind=kLoop, calls=%fused_computation.36 | loop fusion | flops 2193408 | bytes 4369472 | tf_op jit(solution)/shard_map/sub | solution.py:48
  56.5 2.4 %fusion.17 = f32[28,2,2304]{2,1,0:T(2,128)S(1)} fusion(f32[28,2,2304]{2,1,0:T(2,128)S(1)} %fusion.9, f32[28,2,2304]{2,1,0:T(2,128)S(1)} %fusion.13, f32[28,2,2303]{2,1,0:T(2,128)S(1)} %get-tuple-element.33, f32[28,2,2303]{2,1,0:T(2,128)S(1)} %get-tuple-element.32, f32[28,2,2256]{2,1,0:T(2,128)S(1)} %get-tuple-element.31, ...), kind=kLoop, calls=%fused_computation.40 | loop fusion | flops 2193408 | bytes 4369472 | tf_op jit(solution)/shard_map/sub | solution.py:48
  60.5 2.1 %fusion.21 = f32[28,2,2304]{2,1,0:T(2,128)S(1)} fusion(f32[28,2,2304]{2,1,0:T(2,128)S(1)} %fusion.13, f32[28,2,2304]{2,1,0:T(2,128)S(1)} %fusion.17, f32[28,2,2303]{2,1,0:T(2,128)S(1)} %get-tuple-element.27, f32[28,2,2303]{2,1,0:T(2,128)S(1)} %get-tuple-element.26, f32[28,2,2256]{2,1,0:T(2,128)S(1)} %get-tuple-element.25, ...), kind=kLoop, calls=%fused_computation.44 | loop fusion | flops 2193408 | bytes 4369472 | tf_op jit(solution)/shard_map/sub | solution.py:48
  64.2 2.1 %fusion.25 = f32[28,2,2304]{2,1,0:T(2,128)S(1)} fusion(f32[28,2,2304]{2,1,0:T(2,128)S(1)} %fusion.17, f32[28,2,2304]{2,1,0:T(2,128)S(1)} %fusion.21, f32[28,2,2303]{2,1,0:T(2,128)S(1)} %get-tuple-element.21, f32[28,2,2303]{2,1,0:T(2,128)S(1)} %get-tuple-element.20, f32[28,2,2256]{2,1,0:T(2,128)S(1)} %get-tuple-element.19, ...), kind=kLoop, calls=%fused_computation.48 | loop fusion | flops 2193408 | bytes 4369472 | tf_op jit(solution)/shard_map/sub | solution.py:48
  68.0 2.7 %multiply_reduce_fusion.1 = (f32[28]{0:T(128)S(1)}, f32[28,2,2304]{2,1,0:T(2,128)S(1)}) fusion(f32[28,2,2304]{2,1,0:T(2,128)S(1)} %fusion.21, f32[28,2,2304]{2,1,0:T(2,128)S(1)} %fusion.25, bf16[24,2,2304]{2,1,0:T(2,128)(2,1)S(1)} %broadcast_select_fusion.9, bf16[4,2,2304]{2,1,0:T(2,128)(2,1)S(1)} %broadcast_in_dim.216, ...), kind=kLoop, calls=%fused_computation.54 | loop fusion | flops 2451428 | bytes 4369584 | tf_op jit(solution)/shard_map/reduce_sum | solution.py:49
  71.0 1.8 %gather_fusion.3 = bf16[64,2,2304]{2,1,0:T(2,128)(2,1)S(1)} fusion(bf16[28,2,2304]{2,1,0:T(2,128)(2,1)S(1)} %multiply_convert_fusion, s32[1024]{0:T(1024)S(1)} %pad_clamp_fusion.1), kind=kCustom, calls=%fused_computation.3 | custom fusion | bytes 1179904 | tf_op jit(solution)/shard_map/jit(_take)/gather | solution.py:103
  72.8 1.6 %broadcast_select_fusion.5 = bf16[8,8,2,2304]{3,2,1,0:T(2,128)(2,1)} fusion(pred[8,8]{1,0:T(8,128)(4,1)S(1)} %get-tuple-element.65, bf16[8,8,2,2304]{3,2,1,0:T(2,128)(2,1)S(1)} %bitcast.61, pred[8,8]{1,0:T(8,128)(4,1)S(1)} %get-tuple-element.64), kind=kLoop, calls=%fused_computation.19 | loop fusion | flops 589824 | bytes 1179776 | tf_op jit(solution)/shard_map/jit(_where)/select_n | solution.py:106
  74.4 3.5 %all-to-all-start.1 = ((bf16[8,8,2,2304]{3,2,1,0:T(2,128)(2,1)}), bf16[8,8,2,2304]{3,2,1,0:T(2,128)(2,1)S(1)}, u32[]{:S(2)}, u32[]{:S(2)}) async-start(bf16[8,8,2,2304]{3,2,1,0:T(2,128)(2,1)} %broadcast_select_fusion.5), calls=%async_computation.1 | async-start | bytes 1179648 | tf_op jit(solution)/shard_map/all_to_all | solution.py:107
  79.4 0.7 fusion.61
  80.1 0.7 compare_and_fusion.4
  80.8 7.5 %all-to-all-done.1 = bf16[8,8,2,2304]{3,2,1,0:T(2,128)(2,1)S(1)} async-done(((bf16[8,8,2,2304]{3,2,1,0:T(2,128)(2,1)}), bf16[8,8,2,2304]{3,2,1,0:T(2,128)(2,1)S(1)}, u32[]{:S(2)}, u32[]{:S(2)}) %all-to-all-start.1) | async-done | bytes 589856 | tf_op jit(solution)/shard_map/all_to_all | solution.py:107
  88.3 0.8 pad_maximum_fusion
  89.1 1.8 %gather_fusion.4 = bf16[64,2,2304]{2,1,0:T(2,128)(2,1)S(1)} fusion(bf16[68,2,2304]{2,1,0:T(2,128)(2,1)S(1)} %pad_maximum_fusion, s32[1024]{0:T(1024)S(1)} %pad_clamp_fusion), kind=kCustom, calls=%fused_computation.4 | custom fusion | bytes 1179904 | tf_op jit(solution)/shard_map/jit(_take)/gather | solution.py:119
  90.9 1.0 multiply_reduce_fusion
  92.0 4.0 %collective-permute-done = f32[1,2304]{1,0:T(1,128)S(1)} collective-permute-done((f32[1,2304]{1,0:T(1,128)S(1)}, f32[1,2304]{1,0:T(1,128)S(1)}, u32[]{:S(2)}, u32[]{:S(2)}) %collective-permute-start) | collective-permute-done | bytes 9248 | tf_op jit(solution)/shard_map/ppermute | solution.py:20
  96.0 1.5 %copy.6 = f32[1,2304]{0,1:T(8,128)} copy(f32[1,2304]{1,0:T(1,128)S(1)} %slice_add_fusion) | data formatting | bytes 18432
  97.5 1.6 %broadcast_select_fusion.1 = bf16[1,1,64,2,2304]{4,3,2,1,0:T(2,128)(2,1)} fusion(pred[64]{0:T(512)(128)(4,1)S(1)} %iota_compare_fusion.1, bf16[64,2,2304]{2,1,0:T(2,128)(2,1)S(1)} %gather_fusion.4, pred[64]{0:T(512)(128)(4,1)S(1)} %compare_and_fusion.4), kind=kLoop, calls=%fused_computation.15 | loop fusion | flops 589824 | bytes 1179776 | tf_op jit(solution)/shard_map/jit(_where)/select_n | solution.py:120
  99.0 27.1 %reduce-scatter.4.cloned.1.call-done = f32[576,1]{1,0:T(8,128)} async-done(((f32[2304,1]{1,0:T(8,128)}), f32[576,1]{1,0:T(8,128)}) %reduce-scatter.4.cloned.1.call-update) | async-done | bytes 2320
  126.1 1.7 %copy.7 = f32[1,576]{1,0:T(1,128)} copy(f32[1,576]{0,1:T(8,128)} %bitcast.65) | data formatting | bytes 4608
  (70 shorter events, 17.3 us)
Async XLA Ops:
  14.8 7.2 %copy-start = (bf16[1,2304]{1,0:T(2,128)(2,1)S(1)}, bf16[1,2304]{1,0:T(2,128)(2,1)}, u32[]{:S(2)}) copy-start(bf16[1,2304]{1,0:T(2,128)(2,1)} %param.5) | copy-start | bytes 13828
  16.4 21.4 %all-to-all-start = ((bf16[8,8,2,2304]{3,2,1,0:T(2,128)(2,1)}), bf16[8,8,2,2304]{3,2,1,0:T(2,128)(2,1)S(1)}, u32[]{:S(2)}, u32[]{:S(2)}) async-start(bf16[8,8,2,2304]{3,2,1,0:T(2,128)(2,1)} %broadcast_select_fusion.7), calls=%async_computation | async-start | bytes 1179648 | tf_op jit(solution)/shard_map/all_to_all | solution.py:87
  74.4 13.9 %all-to-all-start.1 = ((bf16[8,8,2,2304]{3,2,1,0:T(2,128)(2,1)}), bf16[8,8,2,2304]{3,2,1,0:T(2,128)(2,1)S(1)}, u32[]{:S(2)}, u32[]{:S(2)}) async-start(bf16[8,8,2,2304]{3,2,1,0:T(2,128)(2,1)} %broadcast_select_fusion.5), calls=%async_computation.1 | async-start | bytes 1179648 | tf_op jit(solution)/shard_map/all_to_all | solution.py:107
  77.9 48.2 %reduce-scatter.4.cloned.1.call-start = ((), (), s32[]{:S(2)}) async-start(), calls=%async_computation.3 | async-start | bytes 1474560
  91.9 4.0 %collective-permute-start = (f32[1,2304]{1,0:T(1,128)S(1)}, f32[1,2304]{1,0:T(1,128)S(1)}, u32[]{:S(2)}, u32[]{:S(2)}) collective-permute-start(f32[1,2304]{1,0:T(1,128)S(1)} %slice.280), channel_id=1, source_target_pairs={{7,0},{0,1},{1,2},{2,3},{3,4},{4,5},{5,6},{6,7},{15,8},{8,9},{9,10... | collective-permute-start | bytes 27656 | tf_op jit(solution)/shard_map/ppermute | solution.py:20
Sparse Core Ops, SparseCore 0:
  97.6 28.5 reduce-scatter.3
where the time goes:
time: 135 us
  waiting for transfers between devices  38.6 us (29%)
  other arithmetic  32.6 us (24%)
  local copies, waits for them, and re-layouts  25.3 us (19%)
  between operations  15.6 us (12%)
  blocking collectives  13.5 us (10%)
  starting transfers between devices  9.07 us (7%)
    unnamed x2, waiting for transfers between devices  27.1 us
    all_gather x1, blocking collectives, on_device(): full_line = lax.all_gather(potential, 'dev', axis=0, tiled=True)  13.5 us
    sub x6, other arithmetic, chebyshev_rows(): previous, current = (current, 2.0 * step_map(current, patches) - previous)  13.3 us
    all_to_all x1, waiting for transfers between devices, on_device(): lax.all_to_all(send_back, 'dev', split_axis=0, concat_axis=0, tiled=True)  7.47 us
    all_to_all x1, starting transfers between devices, on_device(): lax.all_to_all(outgoing, 'dev', split_axis=0, concat_axis=0, tiled=True)  5.17 us
    slice x8, local copies, waits for them, and re-layouts, beside_sum(): upper = jnp.concatenate([field[:, :, 1:], edge_z], 2)  4.8 us
    slice x8, local copies, waits for them, and re-layouts, beside_sum(): field[:, :, BZ:]  4.77 us
    ppermute x1, waiting for transfers between devices, from_behind(): return lax.ppermute(block, axis, route)  3.97 us
  transfers between devices with their start and end apart: 4, of which 3 were waited for; matrix products, arithmetic and copies ran while one was open for 4% of the time, Pallas kernels for 0%

commit v1 on v0

v1 whole, which is shorter than its diff:
```python
import functools

import jax
import jax.numpy as jnp
from jax import lax
from jax.experimental import pallas as pl
from jax.experimental.pallas import tpu as pltpu
from jax.sharding import PartitionSpec as P

DEGREE = 8
BZ = 48
SUB = 8

filter_centre = 9.0
filter_half = 7.0


def filter_kernel(scalars, orbital_ref, patch_ref, filtered_ref, density_ref, plain, diagonal, one, two):
    rows, cells = orbital_ref.shape
    slots = rows // 2
    chunk = 256
    strips = BZ // SUB
    planes_y = cells // BZ
    count, parity = scalars[0], scalars[1]

    eye = (
        lax.broadcasted_iota(jnp.int32, (chunk, chunk), 0)
        == lax.broadcasted_iota(jnp.int32, (chunk, chunk), 1)
    ).astype(jnp.float32).astype(jnp.bfloat16)
    across = (((1,), (1,)), ((), ()))

    for start in range(0, cells, chunk):
        plain[pl.ds(start, chunk), :] = lax.dot_general(
            eye, orbital_ref[:, start : start + chunk], across, preferred_element_type=jnp.float32
        )
        near = jnp.broadcast_to(patch_ref[0:1, start : start + chunk], (slots, chunk))
        far = jnp.broadcast_to(patch_ref[1:2, start : start + chunk], (slots, chunk))
        potential = lax.dot_general(
            eye, jnp.concatenate([near, far], 0), across, preferred_element_type=jnp.float32
        )
        diagonal[pl.ds(start, chunk), :] = potential + (6.0 - filter_centre)
    zeros = jnp.zeros((BZ, rows), jnp.float32)
    plain[pl.ds(cells, BZ), :] = zeros
    one[pl.ds(cells, BZ), :] = zeros
    two[pl.ds(cells, BZ), :] = zeros

    sub_ids = lax.broadcasted_iota(jnp.int32, (SUB, rows), 0)

    def strided(ref, y):
        return jnp.concatenate(
            [ref[pl.ds(y * BZ + zi, SUB, stride=strips), :] for zi in range(strips)], 0
        )

    def packed(ref, y):
        return ref[pl.ds(y * BZ, BZ), :]

    def around(before, here, after):
        up = jnp.where(sub_ids == 0, 0.0, pltpu.roll(here[BZ - SUB :], 1, 0))
        down = jnp.where(sub_ids == SUB - 1, 0.0, pltpu.roll(here[:SUB], SUB - 1, 0))
        along_z = jnp.concatenate([up, here[: BZ - SUB]], 0) + jnp.concatenate([here[SUB:], down], 0)
        return along_z + (before + after) + pltpu.roll(here, slots, 1)

    def sweep(load, finish):
        def body(y, carry):
            before, here = carry
            after = load(y + 1)
            finish(y, here, around(before, here, after))
            return here, after

        lax.fori_loop(0, planes_y, body, (zeros, load(0)), unroll=4)

    def first(y, here, beside):
        factor = strided(diagonal, y)
        one[pl.ds(y * BZ, BZ), :] = (factor * here - beside) * (1.0 / filter_half)
        two[pl.ds(y * BZ, BZ), :] = here

    sweep(functools.partial(strided, plain), first)

    scale = 2.0 / filter_half

    def later(source, target):
        def finish(y, here, beside):
            factor = strided(diagonal, y)
            target[pl.ds(y * BZ, BZ), :] = (factor * here - beside) * scale - packed(target, y)

        sweep(functools.partial(packed, source), finish)

    def pair(_, carry):
        later(one, two)
        later(two, one)
        return carry

    lax.fori_loop(0, (DEGREE - 2) // 2, pair, 0)

    def last_body(y, carry):
        before, here, total = carry
        after = packed(one, y + 1)
        beside = around(before, here, after)
        value = (strided(diagonal, y) * here - beside) * scale - packed(two, y)
        for zi in range(strips):
            plain[pl.ds(y * BZ + zi, SUB, stride=strips), :] = value[zi * SUB : (zi + 1) * SUB]
        return here, after, total + value * value

    _, _, total = lax.fori_loop(0, planes_y, last_body, (zeros, packed(one, 0), zeros), unroll=4)
    lane_sum = jnp.sum(total, axis=0, keepdims=True)
    lane_sum = jnp.broadcast_to(lane_sum, (SUB, rows))
    mean_square = (lane_sum + pltpu.roll(lane_sum, slots, 1)) * (1.0 / (2 * cells))
    slot_ids = lax.broadcasted_iota(jnp.int32, (SUB, rows), 1) % slots
    factor = jnp.where(slot_ids < count, lax.rsqrt(mean_square + 1e-06), 0.0)[:1]
    signed = (1.0 - 2.0 * parity.astype(jnp.float32)) / slots

    for start in range(0, cells, chunk):
        rounded = (plain[pl.ds(start, chunk), :] * factor).astype(jnp.bfloat16)
        turned = lax.dot_general(
            eye[:rows, :rows], rounded, across, preferred_element_type=jnp.float32
        )
        filtered_ref[:, start : start + chunk] = turned.astype(jnp.bfloat16)
        squares = turned * turned
        density_ref[0:1, start : start + chunk] = jnp.sum(squares[:slots], axis=0, keepdims=True) * signed
        density_ref[1:2, start : start + chunk] = jnp.sum(squares[slots:], axis=0, keepdims=True) * signed


def filter_box(scalars, orbital_rows, patch):
    rows, cells = orbital_rows.shape
    padded = pltpu.VMEM((cells + BZ, rows), jnp.float32)
    return pl.pallas_call(
        filter_kernel,
        out_shape=(
            jax.ShapeDtypeStruct((rows, cells), jnp.bfloat16),
            jax.ShapeDtypeStruct((2, cells), jnp.float32),
        ),
        in_specs=[
            pl.BlockSpec(memory_space=pltpu.SMEM),
            pl.BlockSpec(memory_space=pltpu.VMEM),
            pl.BlockSpec(memory_space=pltpu.VMEM),
        ],
        out_specs=(
            pl.BlockSpec(memory_space=pltpu.VMEM),
            pl.BlockSpec(memory_space=pltpu.VMEM),
        ),
        scratch_shapes=[padded, pltpu.VMEM((cells, rows), jnp.float32), padded, padded],
        compiler_params=pltpu.CompilerParams(vmem_limit_bytes=16 * 2**20),
        name="filter_box",
    )(scalars, orbital_rows, patch)


def sum_over(part, axis):
    size = lax.axis_size(axis)
    if size & (size - 1):
        return lax.psum_scatter(part, axis, scatter_dimension=0, tiled=True)
    me = lax.axis_index(axis)
    span = size // 2
    while span:
        halves = part.reshape(2, -1)
        mine = (me // span) % 2
        kept = jnp.where(mine == 0, halves[0], halves[1])
        sent = jnp.where(mine == 0, halves[1], halves[0])
        part = kept + lax.ppermute(sent, axis, [(i, i ^ span) for i in range(size)])
        span //= 2
    return part


def on_device(orbitals, potential, counts, parity):
    group_size = lax.axis_size("dev")
    me = lax.axis_index("dev")
    slots, _, cells = orbitals.shape[2:]
    following = lax.ppermute(potential, "dev", [((i + 1) % group_size, i) for i in range(group_size)])
    patch = jnp.concatenate([potential, following], 0)
    orbital_rows = jnp.swapaxes(orbitals[0, 0], 0, 1).reshape(2 * slots, cells)
    count = lax.dynamic_index_in_dim(counts[0], me, 0, keepdims=False)
    scalars = jnp.stack([count, parity[0, 0]])
    filtered_rows, halves = filter_box(scalars, orbital_rows, patch)
    carried = lax.ppermute(halves[1], "dev", [(i, (i + 1) % group_size) for i in range(group_size)])
    density = sum_over(halves[0] + carried, "grp")
    filtered = jnp.swapaxes(filtered_rows.reshape(2, slots, cells), 0, 1)
    return density[None, None], filtered[None, None]


def solution(mesh):
    placed = (P("grp", "dev", None, None, None), P("dev", None), P("grp", None), P("grp", "dev"))
    return jax.shard_map(
        on_device,
        mesh=mesh,
        in_specs=placed,
        out_specs=(P("dev", None, "grp"), P("grp", "dev", None, None, None)),
        check_vma=False,
    )
```

time: 135 us -> 31.5 us (0.23)
  waiting for transfers between devices: 38.6 us -> 6.54 us
  other arithmetic: 32.6 us -> 0.91 us
  local copies, waits for them, and re-layouts: 25.3 us -> 3.79 us
  between operations: 15.6 us -> 1.39 us
  blocking collectives: 13.5 us -> 0 us
  Pallas kernels: 0 us -> 11 us
  starting transfers between devices: 9.07 us -> 7.68 us
    unnamed x2 -> x0, waiting for transfers between devices: 27.1 us -> none
    sub x8 -> x0, other arithmetic: 14.6 us -> none  [the longest x6 13.3 us: chebyshev_rows(): previous, current = (current, 2.0 * step_map(current, patches) - previous)]
    slice x28 -> x1, local copies, waits for them, and re-layouts: 13.6 us -> 0.05 us  [on_device(): halves[1]]
    all_gather x1 -> x0, blocking collectives: 13.5 us -> none  [on_device(): full_line = lax.all_gather(potential, 'dev', axis=0, tiled=True)]
    pallas_call x0 -> x1, Pallas kernels: none -> 11 us  [filter_box(): pl.pallas_call(filter_kernel, out_shape=(jax.ShapeDtypeStruct((rows, cell...]
    all_to_all x2 -> x0, starting transfers between devices: 8.71 us -> none  [the longest x1 5.17 us: on_device(): lax.all_to_all(outgoing, 'dev', split_axis=0, concat_axis=0, tiled=True)]
    gather x6 -> x0, local copies, waits for them, and re-layouts: 8.19 us -> none  [the longest x1 2.84 us: on_device(): jnp.take(orbital_rows, source, axis=0)]
    ppermute x1 -> x4, starting transfers between devices: 0.06 us -> 7.68 us  [the longest x2 4.23 us: sum_over(): part = kept + lax.ppermute(sent, axis, [(i, i ^ span) for i in range(size)])]
  transfers between devices with their start and end apart: 4 -> 4, of which waited for: 3 -> 3; matrix products, arithmetic and copies ran while one was open for 4% -> 12% of each run, Pallas kernels for 0% -> 0%
where the time goes in v1:
time: 31.5 us; the launch traced here: 31.3 us
  Pallas kernels  11 us (35%)
  starting transfers between devices  7.68 us (24%)
  waiting for transfers between devices  6.54 us (21%)
  local copies, waits for them, and re-layouts  3.79 us (12%)
  between operations  1.39 us (4%)
  other arithmetic  0.91 us (3%)
    pallas_call x1, Pallas kernels, filter_box(): pl.pallas_call(filter_kernel, out_shape=(jax.ShapeDtypeStruct((rows, cell...  11 us
    ppermute x2, starting transfers between devices, sum_over(): part = kept + lax.ppermute(sent, axis, [(i, i ^ span) for i in range(size)])  4.23 us
    ppermute x1, waiting for transfers between devices, on_device(): lax.ppermute(halves[1], 'dev', [(i, (i + 1) % group_size) for i in range(...  3.98 us
    ppermute x1, starting transfers between devices, on_device(): lax.ppermute(potential, 'dev', [((i + 1) % group_size, i) for i in range(...  3.39 us
    ppermute x2, waiting for transfers between devices, sum_over(): part = kept + lax.ppermute(sent, axis, [(i, i ^ span) for i in range(size)])  2.57 us
    reshape x1, local copies, waits for them, and re-layouts, on_device(): filtered = jnp.swapaxes(filtered_rows.reshape(2, slots, cells), 0, 1)  1.42 us
    transpose x1, local copies, waits for them, and re-layouts, on_device(): orbital_rows = jnp.swapaxes(orbitals[0, 0], 0, 1).reshape(2 * slots, cells)  1.14 us
    another operation x1, other arithmetic, on_device(): scalars = jnp.stack([count, parity[0, 0]])  0.72 us
  transfers between devices with their start and end apart: 4, of which 3 were waited for; matrix products, arithmetic and copies ran while one was open for 12% of the time, Pallas kernels for 0%

profile of v1, /device:TPU:0, one launch (start us, length us, event | category | flops | bytes accessed | tf_op | source)
XLA Modules:
  0.0 31.3 jit_solution(14952539407828344682)
XLA Ops:
  0.6 0.0 copy-start
  0.6 3.4 %collective-permute-start = (bf16[1,2304]{1,0:T(2,128)(2,1)}, bf16[1,2304]{1,0:T(2,128)(2,1)S(1)}, u32[]{:S(2)}, u32[]{:S(2)}) collective-permute-start(bf16[1,2304]{1,0:T(2,128)(2,1)} %param.5), channel_id=1, source_target_pairs={{1,0},{2,1},{3,2},{4,3},{5,4},{6,5},{7,6},{0,7},{9,8},{10,9},{11,1... | collective-permute-start | bytes 13832 | tf_op jit(solution)/shard_map/ppermute | solution.py:167
  4.7 0.0 copy-done
  4.7 0.6 %constant_dynamic-slice_fusion = s32[1,1]{1,0:T(1,128)} fusion(s32[1,8]{1,0:T(1,128)S(1)} %copy-done, s32[]{:T(128)S(6)} %select_n.49), kind=kLoop, calls=%fused_computation.9 | loop fusion | bytes 12 | tf_op jit(solution)/shard_map/jit(dynamic_index_in_dim)/dynamic_slice | solution.py:170
  5.3 0.7 %pad_add_fusion.scalars = s32[2]{0:T(128)S(1)} fusion(s32[1]{0:T(128)} %bitcast.12, s32[1]{0:T(128)} %bitcast), kind=kLoop, calls=%fused_computation.8 | loop fusion | flops 2 | bytes 16 | tf_op jit(solution)/shard_map/stack | solution.py:171
  6.0 0.0 copy-start.1
  6.0 1.1 %copy.6 = bf16[2,64,2304]{2,1,0:T(8,128)(2,1)S(1)} copy(bf16[2,64,2304]{2,0,1:T(2,128)(2,1)} %bitcast.15) | data formatting | bytes 1179648 | tf_op jit(solution)/shard_map/transpose | solution.py:169
  7.1 0.0 collective-permute-done
  7.2 0.0 copy-done.1
  7.2 11.0 %filter_box.1 = (bf16[128,2304]{1,0:T(8,128)(2,1)S(1)}, f32[2,2304]{1,0:T(2,128)S(1)}) custom-call(s32[2]{0:T(128)S(1)} %pad_add_fusion.scalars, bf16[128,2304]{1,0:T(8,128)(2,1)S(1)} %bitcast.13, bf16[2,2304]{1,0:T(2,128)(2,1)S(1)} %pad_maximum_fusion.patch_ref), custom_call_target="tpu_custom_call" | custom-call | tf_op jit(solution)/shard_map/filter_box/pallas_call | solution.py:126
  18.2 0.1 slice_reduce_fusion
  18.3 0.1 collective-permute-start.1
  18.4 4.0 %collective-permute-done.1 = f32[2304]{0:T(1024)S(1)} collective-permute-done((f32[2304]{0:T(1024)S(1)}, f32[2304]{0:T(1024)S(1)}, u32[]{:S(2)}, u32[]{:S(2)}) %collective-permute-start.1) | collective-permute-done | bytes 9248 | tf_op jit(solution)/shard_map/ppermute | solution.py:173
  22.4 2.7 %collective-permute-start.2 = (f32[1152]{0:T(1024)S(1)}, f32[1152]{0:T(1024)S(1)}, u32[]{:S(2)}, u32[]{:S(2)}) collective-permute-start(f32[1152]{0:T(1024)S(1)} %slice_select_fusion), channel_id=1, source_target_pairs={{0,16},{8,24},{16,0},{24,8},{1,17},{9,25},{17,1},{25,9},{2,18},{10... | collective-permute-start | bytes 13832 | tf_op jit(solution)/shard_map/ppermute | solution.py:158
  25.0 2.0 %collective-permute-done.2 = f32[1152]{0:T(1024)S(1)} collective-permute-done((f32[1152]{0:T(1024)S(1)}, f32[1152]{0:T(1024)S(1)}, u32[]{:S(2)}, u32[]{:S(2)}) %collective-permute-start.2) | collective-permute-done | bytes 4640 | tf_op jit(solution)/shard_map/ppermute | solution.py:158
  27.0 0.1 slice_select_fusion.1
  27.1 1.6 %collective-permute-start.3 = (f32[576]{0:T(1024)S(1)}, f32[576]{0:T(1024)S(1)}, u32[]{:S(2)}, u32[]{:S(2)}) collective-permute-start(f32[576]{0:T(1024)S(1)} %slice_select_fusion.1), channel_id=1, source_target_pairs={{0,8},{8,0},{16,24},{24,16},{1,9},{9,1},{17,25},{25,17},{2,10},{10... | collective-permute-start | bytes 6920 | tf_op jit(solution)/shard_map/ppermute | solution.py:158
  28.6 1.4 %copy.9 = bf16[2,64,2304]{2,0,1:T(2,128)(2,1)} copy(bf16[2,64,2304]{2,1,0:T(8,128)(2,1)S(1)} %bitcast.14) | data formatting | bytes 1179648 | tf_op jit(solution)/shard_map/reshape | solution.py:175
  30.1 0.6 %collective-permute-done.3 = f32[576]{0:T(1024)S(1)} collective-permute-done((f32[576]{0:T(1024)S(1)}, f32[576]{0:T(1024)S(1)}, u32[]{:S(2)}, u32[]{:S(2)}) %collective-permute-start.3) | collective-permute-done | bytes 2336 | tf_op jit(solution)/shard_map/ppermute | solution.py:158
  30.7 0.1 select_add_fusion.1
  30.7 0.6 %broadcast_in_dim.6 = f32[1,1,576]{2,1,0:T(1,128)} reshape(f32[576]{0:T(1024)S(1)} %select_add_fusion.1) | data formatting | bytes 4608 | tf_op jit(solution)/shard_map/broadcast_in_dim | solution.py:176
  (4 shorter events, 0.0 us)
Async XLA Ops:
  0.6 4.1 %copy-start = (s32[1,8]{1,0:T(1,128)S(1)}, s32[1,8]{1,0:T(1,128)}, u32[]{:S(2)}) copy-start(s32[1,8]{1,0:T(1,128)} %param.6) | copy-start | bytes 100
  0.6 6.5 %collective-permute-start = (bf16[1,2304]{1,0:T(2,128)(2,1)}, bf16[1,2304]{1,0:T(2,128)(2,1)S(1)}, u32[]{:S(2)}, u32[]{:S(2)}) collective-permute-start(bf16[1,2304]{1,0:T(2,128)(2,1)} %param.5), channel_id=1, source_target_pairs={{1,0},{2,1},{3,2},{4,3},{5,4},{6,5},{7,6},{0,7},{9,8},{10,9},{11,1... | collective-permute-start | bytes 13832 | tf_op jit(solution)/shard_map/ppermute | solution.py:167
  6.0 1.2 %copy-start.1 = (bf16[1,2304]{1,0:T(2,128)(2,1)S(1)}, bf16[1,2304]{1,0:T(2,128)(2,1)}, u32[]{:S(2)}) copy-start(bf16[1,2304]{1,0:T(2,128)(2,1)} %param.5) | copy-start | bytes 13828
  18.3 4.1 %collective-permute-start.1 = (f32[2304]{0:T(1024)S(1)}, f32[2304]{0:T(1024)S(1)}, u32[]{:S(2)}, u32[]{:S(2)}) collective-permute-start(f32[2304]{0:T(1024)S(1)} %get-tuple-element.6), channel_id=1, source_target_pairs={{0,1},{1,2},{2,3},{3,4},{4,5},{5,6},{6,7},{7,0},{8,9},{9,10},{10,1... | collective-permute-start | bytes 27656 | tf_op jit(solution)/shard_map/ppermute | solution.py:173
  22.4 4.6 %collective-permute-start.2 = (f32[1152]{0:T(1024)S(1)}, f32[1152]{0:T(1024)S(1)}, u32[]{:S(2)}, u32[]{:S(2)}) collective-permute-start(f32[1152]{0:T(1024)S(1)} %slice_select_fusion), channel_id=1, source_target_pairs={{0,16},{8,24},{16,0},{24,8},{1,17},{9,25},{17,1},{25,9},{2,18},{10... | collective-permute-start | bytes 13832 | tf_op jit(solution)/shard_map/ppermute | solution.py:158
  27.1 3.6 %collective-permute-start.3 = (f32[576]{0:T(1024)S(1)}, f32[576]{0:T(1024)S(1)}, u32[]{:S(2)}, u32[]{:S(2)}) collective-permute-start(f32[576]{0:T(1024)S(1)} %slice_select_fusion.1), channel_id=1, source_target_pairs={{0,8},{8,0},{16,24},{24,16},{1,9},{9,1},{17,25},{25,17},{2,10},{10... | collective-permute-start | bytes 6920 | tf_op jit(solution)/shard_map/ppermute | solution.py:158

commit v2 on v1

v2 whole, which is shorter than its diff:
```python
import functools
import math

import jax
import jax.numpy as jnp
from jax import lax
from jax.experimental import pallas as pl
from jax.experimental.pallas import tpu as pltpu
from jax.sharding import PartitionSpec as P

DEGREE = 8
BZ = 48
SUB = 8
CHUNK = 256

filter_centre = 9.0
filter_half = 7.0

across = (((1,), (1,)), ((), ()))


def leja_roots():
    rest = [math.cos((2 * j - 1) * math.pi / (2 * DEGREE)) for j in range(1, DEGREE + 1)]
    order = [rest.pop(0)]
    while rest:
        best = max(rest, key=lambda root: sum(math.log(abs(root - other)) for other in order))
        rest.remove(best)
        order.append(best)
    return order


SHIFTS = [filter_half * root for root in leja_roots()]
LEADING = 2.0 ** (DEGREE - 1) / filter_half**DEGREE


def identity(size):
    down = lax.broadcasted_iota(jnp.int32, (size, size), 0)
    along = lax.broadcasted_iota(jnp.int32, (size, size), 1)
    return (down == along).astype(jnp.float32).astype(jnp.bfloat16)


def turn_kernel(orbital_ref, plain):
    eye = identity(CHUNK)
    for start in range(0, orbital_ref.shape[1], CHUNK):
        plain[start : start + CHUNK, :] = lax.dot_general(
            eye, orbital_ref[:, start : start + CHUNK], across, preferred_element_type=jnp.float32
        )


def filter_kernel(
    counts_ref, parity_ref, plain, near_ref, far_ref, filtered_ref, first_ref, second_ref, ordered, diagonal, one, two
):
    cells, rows = plain.shape
    slots = rows // 2
    strips = BZ // SUB
    planes_y = cells // BZ
    fragments = lax.broadcasted_iota(jnp.int32, counts_ref.shape, 1)
    mine = jnp.where(fragments == lax.axis_index("dev"), counts_ref[...], 0)
    count = jnp.sum(mine, axis=1, keepdims=True)
    signed = (1.0 - 2.0 * parity_ref[...].astype(jnp.float32)) / slots
    eye = identity(CHUNK)

    for start in range(0, cells, CHUNK):
        near = jnp.broadcast_to(near_ref[0:1, start : start + CHUNK], (slots, CHUNK))
        far = jnp.broadcast_to(far_ref[0:1, start : start + CHUNK], (slots, CHUNK))
        potential = lax.dot_general(
            eye, jnp.concatenate([near, far], 0), across, preferred_element_type=jnp.float32
        )
        diagonal[start : start + CHUNK, :] = potential + (6.0 - filter_centre)

    sub_ids = lax.broadcasted_iota(jnp.int32, (SUB, rows), 0)
    is_first, is_last = sub_ids == 0, sub_ids == SUB - 1

    def strided(ref, y):
        return jnp.concatenate(
            [ref[pl.ds(y * BZ + zi, SUB, stride=strips), :] for zi in range(strips)], 0
        )

    def packed(ref, y):
        return ref[y * BZ : (y + 1) * BZ, :]

    def sweep(load, finish):
        here = load(0)
        corner = jnp.zeros((SUB, rows), jnp.float32)
        slanted_before = here
        for y in range(planes_y):
            after = load(y + 1) if y + 1 < planes_y else jnp.zeros((BZ, rows), jnp.float32)
            lower = jnp.where(is_first, 0.0, pltpu.roll(here[BZ - SUB :], 1, 0))
            slanted = after + jnp.concatenate([lower, here[: BZ - SUB]], 0)
            upper = jnp.where(is_last, corner, pltpu.roll(slanted_before[:SUB], SUB - 1, 0))
            beside = slanted + jnp.concatenate([slanted_before[SUB:], upper], 0)
            finish(y, here, beside + pltpu.roll(here, slots, 1))
            corner, slanted_before, here = here[BZ - SUB :], slanted, after

    def factor_first(y, here, beside):
        weight = strided(diagonal, y)
        ordered[y * BZ : (y + 1) * BZ, :] = weight
        one[y * BZ : (y + 1) * BZ, :] = (weight - SHIFTS[0]) * here - beside

    sweep(functools.partial(strided, plain), factor_first)

    source, target = one, two
    for shift in SHIFTS[1:-1]:

        def factor(y, here, beside, target=target, shift=shift):
            target[y * BZ : (y + 1) * BZ, :] = (packed(ordered, y) - shift) * here - beside

        sweep(functools.partial(packed, source), factor)
        source, target = target, source

    totals = [jnp.zeros((BZ, rows), jnp.float32)]

    def factor_last(y, here, beside):
        value = (packed(ordered, y) - SHIFTS[-1]) * here - beside
        for zi in range(strips):
            diagonal[pl.ds(y * BZ + zi, SUB, stride=strips), :] = value[zi * SUB : (zi + 1) * SUB]
        totals[0] = totals[0] + value * value

    sweep(functools.partial(packed, source), factor_last)

    lane_sum = jnp.broadcast_to(jnp.sum(totals[0], axis=0, keepdims=True), (SUB, rows))
    mean_square = (lane_sum + pltpu.roll(lane_sum, slots, 1)) * (LEADING * LEADING / (2 * cells))
    slot_ids = lax.broadcasted_iota(jnp.int32, (SUB, rows), 1) % slots
    scale = jnp.where(slot_ids < count, LEADING * lax.rsqrt(mean_square + 1e-06), 0.0)[:1]

    for start in range(0, cells, CHUNK):
        rounded = (diagonal[start : start + CHUNK, :] * scale).astype(jnp.bfloat16)
        turned = lax.dot_general(
            eye[:rows, :rows], rounded, across, preferred_element_type=jnp.float32
        )
        filtered_ref[:, start : start + CHUNK] = turned.astype(jnp.bfloat16)
        squares = turned * turned
        first_ref[0:1, start : start + CHUNK] = jnp.sum(squares[:slots], axis=0, keepdims=True) * signed
        second_ref[0:1, start : start + CHUNK] = jnp.sum(squares[slots:], axis=0, keepdims=True) * signed


def turn_orbitals(orbital_rows):
    rows, cells = orbital_rows.shape
    return pl.pallas_call(
        turn_kernel,
        out_shape=jax.ShapeDtypeStruct((cells, rows), jnp.float32),
        in_specs=[pl.BlockSpec(memory_space=pltpu.VMEM)],
        out_specs=pl.BlockSpec(memory_space=pltpu.VMEM),
        compiler_params=pltpu.CompilerParams(vmem_limit_bytes=8 * 2**20),
        name="turn_orbitals",
    )(orbital_rows)


def filter_box(counts, parity, plain, near, far):
    cells, rows = plain.shape
    field = pltpu.VMEM((cells, rows), jnp.float32)
    vmem = pl.BlockSpec(memory_space=pltpu.VMEM)
    half = jax.ShapeDtypeStruct((1, cells), jnp.float32)
    return pl.pallas_call(
        filter_kernel,
        out_shape=(jax.ShapeDtypeStruct((rows, cells), jnp.bfloat16), half, half),
        in_specs=[vmem] * 5,
        out_specs=(vmem, vmem, vmem),
        scratch_shapes=[field, field, field, field],
        compiler_params=pltpu.CompilerParams(vmem_limit_bytes=16 * 2**20),
        name="filter_box",
    )(counts, parity, plain, near, far)


def sum_over(part, axis):
    size = lax.axis_size(axis)
    if size & (size - 1):
        return lax.psum_scatter(part, axis, scatter_dimension=1, tiled=True)
    me = lax.axis_index(axis)
    span = size // 2
    while span:
        half = part.shape[1] // 2
        is_low = (me & span) == 0
        kept = jnp.where(is_low, part[:, :half], part[:, half:])
        sent = jnp.where(is_low, part[:, half:], part[:, :half])
        part = kept + lax.ppermute(sent, axis, [(i, i ^ span) for i in range(size)])
        span //= 2
    return part


def on_device(orbitals, potential, counts, parity):
    group_size = lax.axis_size("dev")
    slots, _, cells = orbitals.shape[2:]
    following = lax.ppermute(potential, "dev", [((i + 1) % group_size, i) for i in range(group_size)])
    orbital_rows = jnp.swapaxes(orbitals[0, 0], 0, 1).reshape(2 * slots, cells)
    plain = turn_orbitals(orbital_rows)
    filtered_rows, first, second = filter_box(counts, parity, plain, potential, following)
    carried = lax.ppermute(second, "dev", [(i, (i + 1) % group_size) for i in range(group_size)])
    density = sum_over(first + carried, "grp")
    filtered = jnp.swapaxes(filtered_rows.reshape(2, slots, cells), 0, 1)
    return density[None], filtered[None, None]


def solution(mesh):
    placed = (P("grp", "dev", None, None, None), P("dev", None), P("grp", None), P("grp", "dev"))
    return jax.shard_map(
        on_device,
        mesh=mesh,
        in_specs=placed,
        out_specs=(P("dev", None, "grp"), P("grp", "dev", None, None, None)),
        check_vma=False,
    )
```

time: 31.5 us -> 23 us (0.73)
  Pallas kernels: 11 us -> 4 us
  local copies, waits for them, and re-layouts: 3.79 us -> 2.56 us
    pallas_call x1, Pallas kernels: 11 us -> 3.54 us  [filter_box(): pl.pallas_call(filter_kernel, out_shape=(jax.ShapeDtypeStruct((rows, cell...]
    another operation x1 -> x0, other arithmetic: 0.72 us -> none  [on_device(): scalars = jnp.stack([count, parity[0, 0]])]
    broadcast_in_dim x0 -> x1, other arithmetic: none -> 0.66 us  [on_device(): return (density[None], filtered[None, None])]
    dynamic_slice x1 -> x0, local copies, waits for them, and re-layouts: 0.59 us -> none  [on_device(): count = lax.dynamic_index_in_dim(counts[0], me, 0, keepdims=False)]
    broadcast_in_dim x1 -> x0, local copies, waits for them, and re-layouts: 0.58 us -> none  [on_device(): return (density[None, None], filtered[None, None])]
    pallas_call x0 -> x1, Pallas kernels: none -> 0.46 us  [turn_orbitals(): pl.pallas_call(turn_kernel, out_shape=jax.ShapeDtypeStruct((cells, rows),...]
  transfers between devices with their start and end apart: 4 -> 4, of which waited for: 3 -> 3; matrix products, arithmetic and copies ran while one was open for 12% -> 11% of each run, Pallas kernels for 0% -> 2%
where the time goes in v2:
time: 23 us; the launch traced here: 22.9 us
  starting transfers between devices  7.72 us (34%)
  waiting for transfers between devices  6.45 us (28%)
  Pallas kernels  4 us (17%)
  local copies, waits for them, and re-layouts  2.56 us (11%)
  between operations  1.38 us (6%)
  other arithmetic  0.76 us (3%)
    ppermute x2, starting transfers between devices, sum_over(): part = kept + lax.ppermute(sent, axis, [(i, i ^ span) for i in range(size)])  4.27 us
    ppermute x1, waiting for transfers between devices, on_device(): lax.ppermute(second, 'dev', [(i, (i + 1) % group_size) for i in range(gro...  3.96 us
    pallas_call x1, Pallas kernels, filter_box(): pl.pallas_call(filter_kernel, out_shape=(jax.ShapeDtypeStruct((rows, cell...  3.54 us
    ppermute x1, starting transfers between devices, on_device(): lax.ppermute(potential, 'dev', [((i + 1) % group_size, i) for i in range(...  3.39 us
    ppermute x2, waiting for transfers between devices, sum_over(): part = kept + lax.ppermute(sent, axis, [(i, i ^ span) for i in range(size)])  2.48 us
    reshape x1, local copies, waits for them, and re-layouts, on_device(): filtered = jnp.swapaxes(filtered_rows.reshape(2, slots, cells), 0, 1)  1.42 us
    transpose x1, local copies, waits for them, and re-layouts, on_device(): orbital_rows = jnp.swapaxes(orbitals[0, 0], 0, 1).reshape(2 * slots, cells)  1.12 us
    broadcast_in_dim x1, other arithmetic, on_device(): return (density[None], filtered[None, None])  0.66 us
  transfers between devices with their start and end apart: 4, of which 3 were waited for; matrix products, arithmetic and copies ran while one was open for 11% of the time, Pallas kernels for 2%

profile of v2, /device:TPU:0, one launch (start us, length us, event | category | flops | bytes accessed | tf_op | source)
XLA Modules:
  0.0 22.9 jit_solution(10240463688353523982)
XLA Ops:
  0.6 3.4 %collective-permute-start = (bf16[1,2304]{1,0:T(2,128)(2,1)}, bf16[1,2304]{1,0:T(2,128)(2,1)S(1)}, u32[]{:S(2)}, u32[]{:S(2)}) collective-permute-start(bf16[1,2304]{1,0:T(2,128)(2,1)} %near_ref.1), channel_id=1, source_target_pairs={{1,0},{2,1},{3,2},{4,3},{5,4},{6,5},{7,6},{0,7},{9,8},{10,9},{11,1... | collective-permute-start | bytes 13832 | tf_op jit(solution)/shard_map/ppermute | solution.py:184
  4.0 1.1 %copy.6 = bf16[2,64,2304]{2,1,0:T(8,128)(2,1)S(1)} copy(bf16[2,64,2304]{2,0,1:T(2,128)(2,1)} %bitcast.14) | data formatting | bytes 1179648 | tf_op jit(solution)/shard_map/transpose | solution.py:185
  5.1 0.0 copy-start
  5.2 0.0 copy-start.1
  5.2 0.5 %turn_orbitals.1.plain = f32[2304,128]{1,0:T(8,128)S(1)} custom-call(bf16[128,2304]{1,0:T(8,128)(2,1)S(1)} %bitcast.12), custom_call_target="tpu_custom_call" | custom-call | tf_op jit(solution)/shard_map/turn_orbitals/pallas_call | solution.py:139
  6.3 0.0 collective-permute-done.far_ref
  6.3 0.0 copy-done
  6.3 0.0 copy-done.1
  6.3 3.5 %filter_box.1 = (bf16[128,2304]{1,0:T(8,128)(2,1)S(1)}, f32[1,2304]{1,0:T(1,128)S(1)}, f32[1,2304]{1,0:T(1,128)S(1)}) custom-call(s32[1,8]{1,0:T(1,128)S(1)} %copy-done.1, s32[1,1]{1,0:T(1,128)S(6)} %copy.10.parity_ref, f32[2304,128]{1,0:T(8,128)S(1)} %turn_orbitals.1.plain, bf16[1,2304]{1,0:T(2,128)(2,1)S(1)} %copy-done, ...), custom_call_target="tpu_custom_call" | custom-call | tf_op jit(solution)/shard_map/filter_box/pallas_call | solution.py:154
  9.9 0.1 collective-permute-start.1
  9.9 4.0 %collective-permute-done.1 = f32[1,2304]{1,0:T(1,128)S(1)} collective-permute-done((f32[1,2304]{1,0:T(1,128)S(1)}, f32[1,2304]{1,0:T(1,128)S(1)}, u32[]{:S(2)}, u32[]{:S(2)}) %collective-permute-start.1) | collective-permute-done | bytes 9248 | tf_op jit(solution)/shard_map/ppermute | solution.py:188
  13.9 2.7 %collective-permute-start.2 = (f32[1,1152]{1,0:T(1,128)S(1)}, f32[1,1152]{1,0:T(1,128)S(1)}, u32[]{:S(2)}, u32[]{:S(2)}) collective-permute-start(f32[1,1152]{1,0:T(1,128)S(1)} %broadcast_select_fusion), channel_id=1, source_target_pairs={{0,16},{8,24},{16,0},{24,8},{1,17},{9,25},{17,1},{25,9},{2,18},{10... | collective-permute-start | bytes 13832 | tf_op jit(solution)/shard_map/ppermute | solution.py:176
  16.6 1.9 %collective-permute-done.2 = f32[1,1152]{1,0:T(1,128)S(1)} collective-permute-done((f32[1,1152]{1,0:T(1,128)S(1)}, f32[1,1152]{1,0:T(1,128)S(1)}, u32[]{:S(2)}, u32[]{:S(2)}) %collective-permute-start.2) | collective-permute-done | bytes 4640 | tf_op jit(solution)/shard_map/ppermute | solution.py:176
  18.5 0.1 broadcast_select_fusion.2
  18.6 1.6 %collective-permute-start.3 = (f32[1,576]{1,0:T(1,128)S(1)}, f32[1,576]{1,0:T(1,128)S(1)}, u32[]{:S(2)}, u32[]{:S(2)}) collective-permute-start(f32[1,576]{1,0:T(1,128)S(1)} %broadcast_select_fusion.2), channel_id=1, source_target_pairs={{0,8},{8,0},{16,24},{24,16},{1,9},{9,1},{17,25},{25,17},{2,10},{10... | collective-permute-start | bytes 6920 | tf_op jit(solution)/shard_map/ppermute | solution.py:176
  20.2 1.4 %copy.9 = bf16[2,64,2304]{2,0,1:T(2,128)(2,1)} copy(bf16[2,64,2304]{2,1,0:T(8,128)(2,1)S(1)} %bitcast.13) | data formatting | bytes 1179648 | tf_op jit(solution)/shard_map/reshape | solution.py:190
  21.6 0.6 %collective-permute-done.3 = f32[1,576]{1,0:T(1,128)S(1)} collective-permute-done((f32[1,576]{1,0:T(1,128)S(1)}, f32[1,576]{1,0:T(1,128)S(1)}, u32[]{:S(2)}, u32[]{:S(2)}) %collective-permute-start.3) | collective-permute-done | bytes 2336 | tf_op jit(solution)/shard_map/ppermute | solution.py:176
  22.2 0.7 %fusion.2 = f32[1,1,576]{2,1,0:T(1,128)} fusion(f32[1,576]{1,0:T(1,128)S(1)} %collective-permute-done.3, pred[]{:T(512)S(6)} %eq.6, f32[1,1152]{1,0:T(1,128)S(1)} %fusion), kind=kLoop, calls=%fused_computation.7 | loop fusion | flops 1152 | bytes 9217 | tf_op jit(solution)/shard_map/broadcast_in_dim | solution.py:191
  (3 shorter events, 0.0 us)
Async XLA Ops:
  0.6 5.7 %collective-permute-start = (bf16[1,2304]{1,0:T(2,128)(2,1)}, bf16[1,2304]{1,0:T(2,128)(2,1)S(1)}, u32[]{:S(2)}, u32[]{:S(2)}) collective-permute-start(bf16[1,2304]{1,0:T(2,128)(2,1)} %near_ref.1), channel_id=1, source_target_pairs={{1,0},{2,1},{3,2},{4,3},{5,4},{6,5},{7,6},{0,7},{9,8},{10,9},{11,1... | collective-permute-start | bytes 13832 | tf_op jit(solution)/shard_map/ppermute | solution.py:184
  5.1 1.2 %copy-start = (bf16[1,2304]{1,0:T(2,128)(2,1)S(1)}, bf16[1,2304]{1,0:T(2,128)(2,1)}, u32[]{:S(2)}) copy-start(bf16[1,2304]{1,0:T(2,128)(2,1)} %near_ref.1) | copy-start | bytes 13828
  5.2 1.2 %copy-start.1 = (s32[1,8]{1,0:T(1,128)S(1)}, s32[1,8]{1,0:T(1,128)}, u32[]{:S(2)}) copy-start(s32[1,8]{1,0:T(1,128)} %counts_ref.1) | copy-start | bytes 100
  9.9 4.0 %collective-permute-start.1 = (f32[1,2304]{1,0:T(1,128)S(1)}, f32[1,2304]{1,0:T(1,128)S(1)}, u32[]{:S(2)}, u32[]{:S(2)}) collective-permute-start(f32[1,2304]{1,0:T(1,128)S(1)} %get-tuple-element.6), channel_id=1, source_target_pairs={{0,1},{1,2},{2,3},{3,4},{4,5},{5,6},{6,7},{7,0},{8,9},{9,10},{10,1... | collective-permute-start | bytes 27656 | tf_op jit(solution)/shard_map/ppermute | solution.py:188
  13.9 4.6 %collective-permute-start.2 = (f32[1,1152]{1,0:T(1,128)S(1)}, f32[1,1152]{1,0:T(1,128)S(1)}, u32[]{:S(2)}, u32[]{:S(2)}) collective-permute-start(f32[1,1152]{1,0:T(1,128)S(1)} %broadcast_select_fusion), channel_id=1, source_target_pairs={{0,16},{8,24},{16,0},{24,8},{1,17},{9,25},{17,1},{25,9},{2,18},{10... | collective-permute-start | bytes 13832 | tf_op jit(solution)/shard_map/ppermute | solution.py:176
  18.6 3.6 %collective-permute-start.3 = (f32[1,576]{1,0:T(1,128)S(1)}, f32[1,576]{1,0:T(1,128)S(1)}, u32[]{:S(2)}, u32[]{:S(2)}) collective-permute-start(f32[1,576]{1,0:T(1,128)S(1)} %broadcast_select_fusion.2), channel_id=1, source_target_pairs={{0,8},{8,0},{16,24},{24,16},{1,9},{9,1},{17,25},{25,17},{2,10},{10... | collective-permute-start | bytes 6920 | tf_op jit(solution)/shard_map/ppermute | solution.py:176

commit v3 on v2

--- a/solution.py
+++ b/solution.py
@@ -39,27 +39,48 @@
     return (down == along).astype(jnp.float32).astype(jnp.bfloat16)
 
 
-def turn_kernel(orbital_ref, plain):
-    eye = identity(CHUNK)
-    for start in range(0, orbital_ref.shape[1], CHUNK):
+def eye_kernel(eye_ref):
+    eye_ref[...] = identity(eye_ref.shape[0])
+
+
+def turn_kernel(orbital_ref, eye_ref, plain):
+    cells, rows = plain.shape
+    for start in range(0, cells, CHUNK):
+        part = jnp.swapaxes(orbital_ref[:, :, start : start + CHUNK], 0, 1)
         plain[start : start + CHUNK, :] = lax.dot_general(
-            eye, orbital_ref[:, start : start + CHUNK], across, preferred_element_type=jnp.float32
+            eye_ref[...], part.reshape(rows, CHUNK), across, preferred_element_type=jnp.float32
         )
 
 
 def filter_kernel(
-    counts_ref, parity_ref, plain, near_ref, far_ref, filtered_ref, first_ref, second_ref, ordered, diagonal, one, two
+    counts_hbm,
+    parity_any,
+    plain,
+    near_ref,
+    far_ref,
+    filtered_ref,
+    halves_ref,
+    counts_ref,
+    parity_ref,
+    ordered,
+    diagonal,
+    one,
+    two,
+    sems,
 ):
     cells, rows = plain.shape
     slots = rows // 2
     strips = BZ // SUB
     planes_y = cells // BZ
-    fragments = lax.broadcasted_iota(jnp.int32, counts_ref.shape, 1)
-    mine = jnp.where(fragments == lax.axis_index("dev"), counts_ref[...], 0)
-    count = jnp.sum(mine, axis=1, keepdims=True)
-    signed = (1.0 - 2.0 * parity_ref[...].astype(jnp.float32)) / slots
+
+    small = [
+        pltpu.make_async_copy(counts_hbm, counts_ref, sems.at[0]),
+        pltpu.make_async_copy(parity_any, parity_ref, sems.at[1]),
+    ]
+    for copy in small:
+        copy.start()
+
     eye = identity(CHUNK)
-
     for start in range(0, cells, CHUNK):
         near = jnp.broadcast_to(near_ref[0:1, start : start + CHUNK], (slots, CHUNK))
         far = jnp.broadcast_to(far_ref[0:1, start : start + CHUNK], (slots, CHUNK))
@@ -118,6 +139,11 @@
 
     sweep(functools.partial(packed, source), factor_last)
 
+    for copy in small:
+        copy.wait()
+    count = counts_ref[0, lax.axis_index("dev")]
+    signed = (1.0 - 2.0 * parity_ref[0, 0].astype(jnp.float32)) / slots
+
     lane_sum = jnp.broadcast_to(jnp.sum(totals[0], axis=0, keepdims=True), (SUB, rows))
     mean_square = (lane_sum + pltpu.roll(lane_sum, slots, 1)) * (LEADING * LEADING / (2 * cells))
     slot_ids = lax.broadcasted_iota(jnp.int32, (SUB, rows), 1) % slots
@@ -130,33 +156,52 @@
         )
         filtered_ref[:, start : start + CHUNK] = turned.astype(jnp.bfloat16)
         squares = turned * turned
-        first_ref[0:1, start : start + CHUNK] = jnp.sum(squares[:slots], axis=0, keepdims=True) * signed
-        second_ref[0:1, start : start + CHUNK] = jnp.sum(squares[slots:], axis=0, keepdims=True) * signed
-
-
-def turn_orbitals(orbital_rows):
-    rows, cells = orbital_rows.shape
+        first = jnp.sum(squares[:slots], axis=0, keepdims=True)
+        second = jnp.sum(squares[slots:], axis=0, keepdims=True)
+        halves_ref[0:1, start : start + CHUNK] = first * signed
+        halves_ref[1:2, start : start + CHUNK] = second * signed
+
+
+def make_eye():
+    return pl.pallas_call(
+        eye_kernel,
+        out_shape=jax.ShapeDtypeStruct((CHUNK, CHUNK), jnp.bfloat16),
+        out_specs=pl.BlockSpec(memory_space=pltpu.VMEM),
+        compiler_params=pltpu.CompilerParams(vmem_limit_bytes=2**20),
+        cost_estimate=pl.CostEstimate(flops=10**10, bytes_accessed=0, transcendentals=0),
+        name="make_eye",
+    )()
+
+
+def turn_orbitals(orbitals, eye):
+    slots, planes, cells = orbitals.shape
+    vmem = pl.BlockSpec(memory_space=pltpu.VMEM)
     return pl.pallas_call(
         turn_kernel,
-        out_shape=jax.ShapeDtypeStruct((cells, rows), jnp.float32),
-        in_specs=[pl.BlockSpec(memory_space=pltpu.VMEM)],
-        out_specs=pl.BlockSpec(memory_space=pltpu.VMEM),
+        out_shape=jax.ShapeDtypeStruct((cells, planes * slots), jnp.float32),
+        in_specs=[vmem, vmem],
+        out_specs=vmem,
         compiler_params=pltpu.CompilerParams(vmem_limit_bytes=8 * 2**20),
         name="turn_orbitals",
-    )(orbital_rows)
+    )(orbitals, eye)
 
 
 def filter_box(counts, parity, plain, near, far):
     cells, rows = plain.shape
     field = pltpu.VMEM((cells, rows), jnp.float32)
-    vmem = pl.BlockSpec(memory_space=pltpu.VMEM)
-    half = jax.ShapeDtypeStruct((1, cells), jnp.float32)
+    vmem, hbm = pl.BlockSpec(memory_space=pltpu.VMEM), pl.BlockSpec(memory_space=pltpu.HBM)
+    counts = pltpu.with_memory_space_constraint(counts, pltpu.HBM)
     return pl.pallas_call(
         filter_kernel,
-        out_shape=(jax.ShapeDtypeStruct((rows, cells), jnp.bfloat16), half, half),
-        in_specs=[vmem] * 5,
-        out_specs=(vmem, vmem, vmem),
-        scratch_shapes=[field, field, field, field],
+        out_shape=(
+            jax.ShapeDtypeStruct((rows, cells), jnp.bfloat16),
+            jax.ShapeDtypeStruct((2, cells), jnp.float32),
+        ),
+        in_specs=[hbm, pl.BlockSpec(memory_space=pl.ANY)] + [vmem] * 3,
+        out_specs=(vmem, vmem),
+        scratch_shapes=[pltpu.SMEM(counts.shape, jnp.int32), pltpu.SMEM(parity.shape, jnp.int32)]
+        + [field] * 4
+        + [pltpu.SemaphoreType.DMA((2,))],
         compiler_params=pltpu.CompilerParams(vmem_limit_bytes=16 * 2**20),
         name="filter_box",
     )(counts, parity, plain, near, far)
@@ -181,12 +226,13 @@
 def on_device(orbitals, potential, counts, parity):
     group_size = lax.axis_size("dev")
     slots, _, cells = orbitals.shape[2:]
-    following = lax.ppermute(potential, "dev", [((i + 1) % group_size, i) for i in range(group_size)])
-    orbital_rows = jnp.swapaxes(orbitals[0, 0], 0, 1).reshape(2 * slots, cells)
-    plain = turn_orbitals(orbital_rows)
-    filtered_rows, first, second = filter_box(counts, parity, plain, potential, following)
-    carried = lax.ppermute(second, "dev", [(i, (i + 1) % group_size) for i in range(group_size)])
-    density = sum_over(first + carried, "grp")
+    far = lax.ppermute(potential, "dev", [((i + 1) % group_size, i) for i in range(group_size)])
+    eye = make_eye()
+    plain = turn_orbitals(orbitals[0, 0], eye)
+    filtered_rows, halves = filter_box(counts, parity, plain, potential, far)
+    halves = sum_over(halves, "grp")
+    onward = [(i, (i + 1) % group_size) for i in range(group_size)]
+    density = halves[:1] + lax.ppermute(halves[1:], "dev", onward)
     filtered = jnp.swapaxes(filtered_rows.reshape(2, slots, cells), 0, 1)
     return density[None], filtered[None, None]
 

time: 23 us -> 22.3 us (0.970)
  local copies, waits for them, and re-layouts: 2.56 us -> 1.44 us
  waiting for transfers between devices: 6.45 us -> 6.78 us
    ppermute x2, waiting for transfers between devices: 2.48 us -> 4.01 us  [sum_over(): part = kept + lax.ppermute(sent, axis, [(i, i ^ span) for i in range(size)])]
    ppermute x1, waiting for transfers between devices: 3.96 us -> 2.48 us  [on_device(): density = halves[:1] + lax.ppermute(halves[1:], 'dev', onward)]
    transpose x1 -> x0, local copies, waits for them, and re-layouts: 1.12 us -> none  [on_device(): orbital_rows = jnp.swapaxes(orbitals[0, 0], 0, 1).reshape(2 * slots, cells)]
    ppermute x1, waiting for transfers between devices: 0.01 us -> 0.29 us  [on_device(): lax.ppermute(potential, 'dev', [((i + 1) % group_size, i) for i in range(...]
    pallas_call x1 -> x2, Pallas kernels: 0.46 us -> 0.6 us  [the longest x1 0.58 us: turn_orbitals(): pl.pallas_call(turn_kernel, out_shape=jax.ShapeDtypeStruct((cells, planes...]
  transfers between devices with their start and end apart: 4 -> 4, of which waited for: 3 -> 4; matrix products, arithmetic and copies ran while one was open for 11% -> 6% of each run, Pallas kernels for 2% -> 3%
where the time goes in v3:
time: 22.3 us; the launch traced here: 22.2 us
  starting transfers between devices  7.69 us (34%)
  waiting for transfers between devices  6.78 us (30%)
  Pallas kernels  4.14 us (19%)
  local copies, waits for them, and re-layouts  1.44 us (6%)
  between operations  1.36 us (6%)
  other arithmetic  0.75 us (3%)
    ppermute x2, starting transfers between devices, sum_over(): part = kept + lax.ppermute(sent, axis, [(i, i ^ span) for i in range(size)])  4.25 us
    ppermute x2, waiting for transfers between devices, sum_over(): part = kept + lax.ppermute(sent, axis, [(i, i ^ span) for i in range(size)])  4.01 us
    pallas_call x1, Pallas kernels, filter_box(): pl.pallas_call(filter_kernel, out_shape=(jax.ShapeDtypeStruct((rows, cell...  3.54 us
    ppermute x1, starting transfers between devices, on_device(): lax.ppermute(potential, 'dev', [((i + 1) % group_size, i) for i in range(...  3.39 us
    ppermute x1, waiting for transfers between devices, on_device(): density = halves[:1] + lax.ppermute(halves[1:], 'dev', onward)  2.48 us
    reshape x1, local copies, waits for them, and re-layouts, on_device(): filtered = jnp.swapaxes(filtered_rows.reshape(2, slots, cells), 0, 1)  1.42 us
    broadcast_in_dim x1, other arithmetic, on_device(): return (density[None], filtered[None, None])  0.58 us
    pallas_call x1, Pallas kernels, turn_orbitals(): pl.pallas_call(turn_kernel, out_shape=jax.ShapeDtypeStruct((cells, planes...  0.58 us
  transfers between devices with their start and end apart: 4, of which 4 were waited for; matrix products, arithmetic and copies ran while one was open for 6% of the time, Pallas kernels for 3%

profile of v3, /device:TPU:0, one launch (start us, length us, event | category | flops | bytes accessed | tf_op | source)
XLA Modules:
  0.0 22.2 jit_solution(848600704456290018)
XLA Ops:
  0.6 0.0 copy-start
  0.6 3.4 %collective-permute-start = (bf16[1,2304]{1,0:T(2,128)(2,1)}, bf16[1,2304]{1,0:T(2,128)(2,1)S(1)}, u32[]{:S(2)}, u32[]{:S(2)}) collective-permute-start(bf16[1,2304]{1,0:T(2,128)(2,1)} %near_ref.1), channel_id=1, source_target_pairs={{1,0},{2,1},{3,2},{4,3},{5,4},{6,5},{7,6},{0,7},{9,8},{10,9},{11,1... | collective-permute-start | bytes 13832 | tf_op jit(solution)/shard_map/ppermute | solution.py:229
  4.1 0.0 copy-start.1
  4.7 0.0 copy-done
  4.7 0.6 %turn_orbitals.1.plain = f32[2304,128]{1,0:T(8,128)S(1)} custom-call(bf16[64,2,2304]{2,1,0:T(2,128)(2,1)S(1)} %bitcast.10, bf16[256,256]{1,0:T(8,128)(2,1)S(1)} %make_eye.1.eye_ref), custom_call_target="tpu_custom_call" | custom-call | tf_op jit(solution)/shard_map/turn_orbitals/pallas_call | solution.py:179
  5.3 0.3 %collective-permute-done.far_ref = bf16[1,2304]{1,0:T(2,128)(2,1)S(1)} collective-permute-done((bf16[1,2304]{1,0:T(2,128)(2,1)}, bf16[1,2304]{1,0:T(2,128)(2,1)S(1)}, u32[]{:S(2)}, u32[]{:S(2)}) %collective-permute-start) | collective-permute-done | bytes 4640 | tf_op jit(solution)/shard_map/ppermute | solution.py:229
  5.6 0.0 copy-done.1
  5.6 3.5 %filter_box.1 = (bf16[128,2304]{1,0:T(8,128)(2,1)S(1)}, f32[2,2304]{1,0:T(2,128)S(1)}) custom-call(s32[1,8]{1,0:T(1,128)} %counts_hbm.1, s32[1,1]{1,0:T(1,128)S(6)} %copy.9.parity_any, f32[2304,128]{1,0:T(8,128)S(1)} %turn_orbitals.1.plain, bf16[1,2304]{1,0:T(2,128)(2,1)S(1)} %copy-done.1, bf16[1,2304]{1,0:T(2,128)(2,1)S(1)} %collective-permute-done.far_ref), custom_call_target="tpu_custom_call" | custom-call | tf_op jit(solution)/shard_map/filter_box/pallas_call | solution.py:194
  9.2 2.7 %collective-permute-start.1 = (f32[2,1152]{1,0:T(2,128)S(1)}, f32[2,1152]{1,0:T(2,128)S(1)}, u32[]{:S(2)}, u32[]{:S(2)}) collective-permute-start(f32[2,1152]{1,0:T(2,128)S(1)} %broadcast_select_fusion), channel_id=1, source_target_pairs={{0,16},{8,24},{16,0},{24,8},{1,17},{9,25},{17,1},{25,9},{2,18},{10... | collective-permute-start | bytes 27656 | tf_op jit(solution)/shard_map/ppermute | solution.py:221
  11.8 2.0 %collective-permute-done.1 = f32[2,1152]{1,0:T(2,128)S(1)} collective-permute-done((f32[2,1152]{1,0:T(2,128)S(1)}, f32[2,1152]{1,0:T(2,128)S(1)}, u32[]{:S(2)}, u32[]{:S(2)}) %collective-permute-start.1) | collective-permute-done | bytes 9248 | tf_op jit(solution)/shard_map/ppermute | solution.py:221
  13.8 0.1 broadcast_select_fusion.1
  13.9 1.6 %collective-permute-start.2 = (f32[2,576]{1,0:T(2,128)S(1)}, f32[2,576]{1,0:T(2,128)S(1)}, u32[]{:S(2)}, u32[]{:S(2)}) collective-permute-start(f32[2,576]{1,0:T(2,128)S(1)} %broadcast_select_fusion.1), channel_id=1, source_target_pairs={{0,8},{8,0},{16,24},{24,16},{1,9},{9,1},{17,25},{25,17},{2,10},{10... | collective-permute-start | bytes 13832 | tf_op jit(solution)/shard_map/ppermute | solution.py:221
  15.5 2.0 %collective-permute-done.2 = f32[2,576]{1,0:T(2,128)S(1)} collective-permute-done((f32[2,576]{1,0:T(2,128)S(1)}, f32[2,576]{1,0:T(2,128)S(1)}, u32[]{:S(2)}, u32[]{:S(2)}) %collective-permute-start.2) | collective-permute-done | bytes 4640 | tf_op jit(solution)/shard_map/ppermute | solution.py:221
  17.5 0.1 select_add_fusion.1
  17.6 0.1 collective-permute-start.3
  17.7 1.4 %copy.8 = bf16[2,64,2304]{2,0,1:T(2,128)(2,1)} copy(bf16[2,64,2304]{2,1,0:T(8,128)(2,1)S(1)} %bitcast.9) | data formatting | bytes 1179648 | tf_op jit(solution)/shard_map/reshape | solution.py:236
  19.1 2.5 %collective-permute-done.3 = f32[1,576]{1,0:T(1,128)S(1)} collective-permute-done((f32[1,576]{1,0:T(1,128)S(1)}, f32[1,576]{1,0:T(1,128)S(1)}, u32[]{:S(2)}, u32[]{:S(2)}) %collective-permute-start.3) | collective-permute-done | bytes 2336 | tf_op jit(solution)/shard_map/ppermute | solution.py:235
  21.6 0.6 %fusion = f32[1,1,576]{2,1,0:T(1,128)} fusion(f32[1,576]{1,0:T(1,128)S(1)} %collective-permute-done.3, f32[2,576]{1,0:T(2,128)S(1)} %select_add_fusion.1), kind=kLoop, calls=%fused_computation.6 | loop fusion | flops 576 | bytes 6912 | tf_op jit(solution)/shard_map/broadcast_in_dim | solution.py:237
  (4 shorter events, 0.0 us)
Async XLA Ops:
  0.6 4.1 %copy-start = (bf16[1,1,64,2,2304]{4,3,2,1,0:T(2,128)(2,1)S(1)}, bf16[1,1,64,2,2304]{4,3,2,1,0:T(2,128)(2,1)}, u32[]{:S(2)}) copy-start(bf16[1,1,64,2,2304]{4,3,2,1,0:T(2,128)(2,1)} %param.4) | copy-start | bytes 1769476
  0.6 5.0 %collective-permute-start = (bf16[1,2304]{1,0:T(2,128)(2,1)}, bf16[1,2304]{1,0:T(2,128)(2,1)S(1)}, u32[]{:S(2)}, u32[]{:S(2)}) collective-permute-start(bf16[1,2304]{1,0:T(2,128)(2,1)} %near_ref.1), channel_id=1, source_target_pairs={{1,0},{2,1},{3,2},{4,3},{5,4},{6,5},{7,6},{0,7},{9,8},{10,9},{11,1... | collective-permute-start | bytes 13832 | tf_op jit(solution)/shard_map/ppermute | solution.py:229
  4.1 1.6 %copy-start.1 = (bf16[1,2304]{1,0:T(2,128)(2,1)S(1)}, bf16[1,2304]{1,0:T(2,128)(2,1)}, u32[]{:S(2)}) copy-start(bf16[1,2304]{1,0:T(2,128)(2,1)} %near_ref.1) | copy-start | bytes 13828
  9.2 4.6 %collective-permute-start.1 = (f32[2,1152]{1,0:T(2,128)S(1)}, f32[2,1152]{1,0:T(2,128)S(1)}, u32[]{:S(2)}, u32[]{:S(2)}) collective-permute-start(f32[2,1152]{1,0:T(2,128)S(1)} %broadcast_select_fusion), channel_id=1, source_target_pairs={{0,16},{8,24},{16,0},{24,8},{1,17},{9,25},{17,1},{25,9},{2,18},{10... | collective-permute-start | bytes 27656 | tf_op jit(solution)/shard_map/ppermute | solution.py:221
  13.9 3.6 %collective-permute-start.2 = (f32[2,576]{1,0:T(2,128)S(1)}, f32[2,576]{1,0:T(2,128)S(1)}, u32[]{:S(2)}, u32[]{:S(2)}) collective-permute-start(f32[2,576]{1,0:T(2,128)S(1)} %broadcast_select_fusion.1), channel_id=1, source_target_pairs={{0,8},{8,0},{16,24},{24,16},{1,9},{9,1},{17,25},{25,17},{2,10},{10... | collective-permute-start | bytes 13832 | tf_op jit(solution)/shard_map/ppermute | solution.py:221
  17.6 4.0 %collective-permute-start.3 = (f32[1,576]{1,0:T(1,128)S(1)}, f32[1,576]{1,0:T(1,128)S(1)}, u32[]{:S(2)}, u32[]{:S(2)}) collective-permute-start(f32[1,576]{1,0:T(1,128)S(1)} %slice.31), channel_id=1, source_target_pairs={{0,1},{1,2},{2,3},{3,4},{4,5},{5,6},{6,7},{7,0},{8,9},{9,10},{10,1... | collective-permute-start | bytes 6920 | tf_op jit(solution)/shard_map/ppermute | solution.py:235

commit v4 on v3

v4 whole, which is shorter than its diff:
```python
import functools
import math

import jax
import jax.numpy as jnp
from jax import lax
from jax.experimental import pallas as pl
from jax.experimental.pallas import tpu as pltpu
from jax.sharding import PartitionSpec as P

DEGREE = 8
BZ = 48
SUB = 8
CHUNK = 128

filter_centre = 9.0
filter_half = 7.0

across = (((1,), (1,)), ((), ()))


def leja_roots():
    rest = [math.cos((2 * j - 1) * math.pi / (2 * DEGREE)) for j in range(1, DEGREE + 1)]
    order = [rest.pop(0)]
    while rest:
        best = max(rest, key=lambda root: sum(math.log(abs(root - other)) for other in order))
        rest.remove(best)
        order.append(best)
    return order


SHIFTS = [filter_half * root for root in leja_roots()]
LEADING = 2.0 ** (DEGREE - 1) / filter_half**DEGREE


def identity(size):
    down = lax.broadcasted_iota(jnp.int32, (size, size), 0)
    along = lax.broadcasted_iota(jnp.int32, (size, size), 1)
    return (down == along).astype(jnp.float32).astype(jnp.bfloat16)


def eye_kernel(eye_ref):
    eye_ref[...] = identity(eye_ref.shape[0])


def half_rows(row_ref, start, slots):
    upper = row_ref.shape[1] // 2 + start
    return [
        jnp.broadcast_to(row_ref[0:1, at : at + CHUNK], (slots, CHUNK)) for at in (start, upper)
    ]


def turn_kernel(orbital_ref, near_ref, eye_ref, plain, near_diagonal):
    slots, _, cells = orbital_ref.shape
    half, rows = cells // 2, 2 * slots
    eye = eye_ref[...]
    for start in range(0, half, CHUNK):
        lower = jnp.swapaxes(orbital_ref[:, :, start : start + CHUNK], 0, 1)
        upper = jnp.swapaxes(orbital_ref[:, :, half + start : half + start + CHUNK], 0, 1)
        parts = [lower[0], upper[0], lower[1], upper[1]] + half_rows(near_ref, start, slots)
        turned = lax.dot_general(
            eye, jnp.concatenate(parts, 0), across, preferred_element_type=jnp.float32
        )
        plain[start : start + CHUNK, :] = turned[:, :rows]
        plain[half + start : half + start + CHUNK, :] = turned[:, rows : 2 * rows]
        near_diagonal[start : start + CHUNK, :] = turned[:, 2 * rows :] + (6.0 - filter_centre)


def filter_kernel(
    counts_hbm,
    parity_any,
    plain,
    near_diagonal,
    far_ref,
    filtered_ref,
    halves_ref,
    counts_ref,
    parity_ref,
    ordered,
    far_diagonal,
    one,
    two,
    final,
    sems,
):
    cells, rows = plain.shape
    slots, half = rows // 2, cells // 2
    strips = BZ // SUB
    height = half // BZ

    small = [
        pltpu.make_async_copy(counts_hbm, counts_ref, sems.at[0]),
        pltpu.make_async_copy(parity_any, parity_ref, sems.at[1]),
    ]
    for copy in small:
        copy.start()

    eye = identity(CHUNK)
    for start in range(0, half, CHUNK):
        potential = lax.dot_general(
            eye,
            jnp.concatenate(half_rows(far_ref, start, slots), 0),
            across,
            preferred_element_type=jnp.float32,
        )
        far_diagonal[start : start + CHUNK, :] = potential + (6.0 - filter_centre)

    sub_ids = lax.broadcasted_iota(jnp.int32, (SUB, rows), 0)
    is_first, is_last = sub_ids == 0, sub_ids == SUB - 1
    is_lower = lax.broadcasted_iota(jnp.int32, (BZ, rows), 1) < slots

    def strided(ref, at):
        return jnp.concatenate(
            [ref[pl.ds(at + zi, SUB, stride=strips), :] for zi in range(strips)], 0
        )

    def packed(ref, at):
        return ref[at : at + BZ, :]

    def lowered(row):
        first = jnp.where(is_first, 0.0, pltpu.roll(row[BZ - SUB :], 1, 0))
        return jnp.concatenate([first, row[: BZ - SUB]], 0)

    def sweep(load, finish):
        here = [load(x * half) for x in range(2)]
        ends = [jnp.where(is_lower, pltpu.roll(row, slots, 1), 0.0) for row in here]
        before = [pltpu.roll(load(x * half + half - BZ), slots, 1) for x in range(2)]
        before = [jnp.where(is_lower, 0.0, row) for row in before]
        slanted = [row + lowered(last) for row, last in zip(here, before)]
        corner = [row[BZ - SUB :] for row in before]
        for y in range(height):
            after = [load(x * half + (y + 1) * BZ) if y + 1 < height else ends[x] for x in range(2)]
            for x in range(2):
                new = after[x] + lowered(here[x])
                upper = jnp.where(is_last, corner[x], pltpu.roll(slanted[x][:SUB], SUB - 1, 0))
                beside = new + jnp.concatenate([slanted[x][SUB:], upper], 0)
                finish(x, y * BZ, here[x], beside + here[1 - x])
                slanted[x] = new
            corner = [row[BZ - SUB :] for row in here]
            here = after

    def factor_first(x, at, here, beside):
        weight = strided((near_diagonal, far_diagonal)[x], at)
        at = x * half + at
        ordered[at : at + BZ, :] = weight
        one[at : at + BZ, :] = (weight - SHIFTS[0]) * here - beside

    sweep(functools.partial(strided, plain), factor_first)

    def pick(pair, shifts):
        shift = jnp.float32(shifts[0])
        for index, other in enumerate(shifts[1:], 1):
            shift = jnp.where(pair == index, jnp.float32(other), shift)
        return shift

    def factor_pair(pair, carry):
        for source, target, shifts in ((one, two, SHIFTS[1:-1:2]), (two, one, SHIFTS[2:-1:2])):
            shift = pick(pair, shifts)

            def factor(x, at, here, beside, target=target, shift=shift):
                at = x * half + at
                target[at : at + BZ, :] = (packed(ordered, at) - shift) * here - beside

            sweep(functools.partial(packed, source), factor)
        return carry

    lax.fori_loop(0, (DEGREE - 2) // 2, factor_pair, 0)

    totals = [jnp.zeros((BZ, rows), jnp.float32)]

    def factor_last(x, at, here, beside):
        at = x * half + at
        value = (packed(ordered, at) - SHIFTS[-1]) * here - beside
        for zi in range(strips):
            final[pl.ds(at + zi, SUB, stride=strips), :] = value[zi * SUB : (zi + 1) * SUB]
        totals[0] = totals[0] + value * value

    sweep(functools.partial(packed, one), factor_last)

    for copy in small:
        copy.wait()
    count = counts_ref[0, lax.axis_index("dev")]
    signed = (1.0 - 2.0 * parity_ref[0, 0].astype(jnp.float32)) / slots

    lane_sum = jnp.broadcast_to(jnp.sum(totals[0], axis=0, keepdims=True), (SUB, rows))
    mean_square = (lane_sum + pltpu.roll(lane_sum, slots, 1)) * (LEADING * LEADING / (2 * cells))
    slot_ids = lax.broadcasted_iota(jnp.int32, (SUB, rows), 1) % slots
    scale = jnp.where(slot_ids < count, LEADING * lax.rsqrt(mean_square + 1e-06), 0.0)[:1]

    wide = 3 * CHUNK if half % (3 * CHUNK) == 0 else CHUNK
    for x in range(2):
        for start in range(0, half, wide):
            at = x * half + start
            rounded = (final[at : at + wide, :] * scale).astype(jnp.bfloat16)
            turned = lax.dot_general(eye, rounded, across, preferred_element_type=jnp.float32)
            rounded = turned.astype(jnp.bfloat16)
            squares = turned * turned
            for part in range(2):
                mine = slice(part * slots, (part + 1) * slots)
                to = slice(part * half + start, part * half + start + wide)
                filtered_ref[x * slots : (x + 1) * slots, to] = rounded[mine]
                halves_ref[x : x + 1, to] = jnp.sum(squares[mine], axis=0, keepdims=True) * signed


def make_eye():
    return pl.pallas_call(
        eye_kernel,
        out_shape=jax.ShapeDtypeStruct((CHUNK, CHUNK), jnp.bfloat16),
        out_specs=pl.BlockSpec(memory_space=pltpu.VMEM),
        compiler_params=pltpu.CompilerParams(vmem_limit_bytes=2**20),
        cost_estimate=pl.CostEstimate(flops=10**10, bytes_accessed=0, transcendentals=0),
        name="make_eye",
    )()


def turn_orbitals(orbitals, near, eye):
    slots, planes, cells = orbitals.shape
    vmem = pl.BlockSpec(memory_space=pltpu.VMEM)
    return pl.pallas_call(
        turn_kernel,
        out_shape=(
            jax.ShapeDtypeStruct((cells, planes * slots), jnp.float32),
            jax.ShapeDtypeStruct((cells // 2, planes * slots), jnp.float32),
        ),
        in_specs=[vmem] * 3,
        out_specs=(vmem, vmem),
        compiler_params=pltpu.CompilerParams(vmem_limit_bytes=8 * 2**20),
        name="turn_orbitals",
    )(orbitals, near, eye)


def filter_box(counts, parity, plain, near_diagonal, far):
    cells, rows = plain.shape
    field, half = pltpu.VMEM((cells, rows), jnp.float32), pltpu.VMEM((cells // 2, rows), jnp.float32)
    vmem, hbm = pl.BlockSpec(memory_space=pltpu.VMEM), pl.BlockSpec(memory_space=pltpu.HBM)
    counts = pltpu.with_memory_space_constraint(counts, pltpu.HBM)
    return pl.pallas_call(
        filter_kernel,
        out_shape=(
            jax.ShapeDtypeStruct((rows, cells), jnp.bfloat16),
            jax.ShapeDtypeStruct((2, cells), jnp.float32),
        ),
        in_specs=[hbm, pl.BlockSpec(memory_space=pl.ANY)] + [vmem] * 3,
        out_specs=(vmem, vmem),
        scratch_shapes=[pltpu.SMEM(counts.shape, jnp.int32), pltpu.SMEM(parity.shape, jnp.int32)]
        + [field, half, field, field, field]
        + [pltpu.SemaphoreType.DMA((2,))],
        compiler_params=pltpu.CompilerParams(vmem_limit_bytes=16 * 2**20),
        name="filter_box",
    )(counts, parity, plain, near_diagonal, far)


def sum_over(part, axis):
    size = lax.axis_size(axis)
    if size & (size - 1):
        return lax.psum_scatter(part, axis, scatter_dimension=1, tiled=True)
    me = lax.axis_index(axis)
    span = size // 2
    while span:
        half = part.shape[1] // 2
        is_low = (me & span) == 0
        kept = jnp.where(is_low, part[:, :half], part[:, half:])
        sent = jnp.where(is_low, part[:, half:], part[:, :half])
        part = kept + lax.ppermute(sent, axis, [(i, i ^ span) for i in range(size)])
        span //= 2
    return part


def on_device(orbitals, potential, counts, parity):
    group_size = lax.axis_size("dev")
    slots, _, cells = orbitals.shape[2:]
    far = lax.ppermute(potential, "dev", [((i + 1) % group_size, i) for i in range(group_size)])
    eye = make_eye()
    plain, near_diagonal = turn_orbitals(orbitals[0, 0], potential, eye)
    filtered_rows, halves = filter_box(counts, parity, plain, near_diagonal, far)
    halves = sum_over(halves, "grp")
    onward = [(i, (i + 1) % group_size) for i in range(group_size)]
    density = halves[:1] + lax.ppermute(halves[1:], "dev", onward)
    filtered = jnp.swapaxes(filtered_rows.reshape(2, slots, cells), 0, 1)
    return density[None], filtered[None, None]


def solution(mesh):
    placed = (P("grp", "dev", None, None, None), P("dev", None), P("grp", None), P("grp", "dev"))
    return jax.shard_map(
        on_device,
        mesh=mesh,
        in_specs=placed,
        out_specs=(P("dev", None, "grp"), P("grp", "dev", None, None, None)),
        check_vma=False,
    )
```

time: 22.3 us -> 21.9 us (0.982)
    pallas_call x1, Pallas kernels: 3.54 us -> 3.1 us  [filter_box(): pl.pallas_call(filter_kernel, out_shape=(jax.ShapeDtypeStruct((rows, cell...]
    pallas_call x1, Pallas kernels: 0.58 us -> 0.82 us  [turn_orbitals(): pl.pallas_call(turn_kernel, out_shape=(jax.ShapeDtypeStruct((cells, plane...]
  transfers between devices with their start and end apart: 4 -> 4, of which waited for: 4 -> 4; matrix products, arithmetic and copies ran while one was open for 6% -> 7% of each run, Pallas kernels for 3% -> 4%
where the time goes in v4:
time: 21.9 us; the launch traced here: 21.7 us
  starting transfers between devices  7.69 us (35%)
  waiting for transfers between devices  6.56 us (30%)
  Pallas kernels  3.93 us (18%)
  local copies, waits for them, and re-layouts  1.44 us (7%)
  between operations  1.36 us (6%)
  other arithmetic  0.75 us (3%)
    ppermute x2, starting transfers between devices, sum_over(): part = kept + lax.ppermute(sent, axis, [(i, i ^ span) for i in range(size)])  4.24 us
    ppermute x2, waiting for transfers between devices, sum_over(): part = kept + lax.ppermute(sent, axis, [(i, i ^ span) for i in range(size)])  4.01 us
    ppermute x1, starting transfers between devices, on_device(): lax.ppermute(potential, 'dev', [((i + 1) % group_size, i) for i in range(...  3.39 us
    pallas_call x1, Pallas kernels, filter_box(): pl.pallas_call(filter_kernel, out_shape=(jax.ShapeDtypeStruct((rows, cell...  3.1 us
    ppermute x1, waiting for transfers between devices, on_device(): density = halves[:1] + lax.ppermute(halves[1:], 'dev', onward)  2.48 us
    reshape x1, local copies, waits for them, and re-layouts, on_device(): filtered = jnp.swapaxes(filtered_rows.reshape(2, slots, cells), 0, 1)  1.42 us
    pallas_call x1, Pallas kernels, turn_orbitals(): pl.pallas_call(turn_kernel, out_shape=(jax.ShapeDtypeStruct((cells, plane...  0.82 us
    broadcast_in_dim x1, other arithmetic, on_device(): return (density[None], filtered[None, None])  0.58 us
  transfers between devices with their start and end apart: 4, of which 4 were waited for; matrix products, arithmetic and copies ran while one was open for 7% of the time, Pallas kernels for 4%

profile of v4, /device:TPU:0, one launch (start us, length us, event | category | flops | bytes accessed | tf_op | source)
XLA Modules:
  0.0 21.7 jit_solution(9724972950283562268)
XLA Ops:
  0.6 0.0 copy-start.1
  0.6 0.0 copy-start
  0.6 3.4 %collective-permute-start = (bf16[1,2304]{1,0:T(2,128)(2,1)}, bf16[1,2304]{1,0:T(2,128)(2,1)S(1)}, u32[]{:S(2)}, u32[]{:S(2)}) collective-permute-start(bf16[1,2304]{1,0:T(2,128)(2,1)} %near_ref.1), channel_id=1, source_target_pairs={{1,0},{2,1},{3,2},{4,3},{5,4},{6,5},{7,6},{0,7},{9,8},{10,9},{11,1... | collective-permute-start | bytes 13832 | tf_op jit(solution)/shard_map/ppermute | solution.py:272
  4.7 0.0 copy-done.1
  4.7 0.0 copy-done
  4.7 0.8 %turn_orbitals.1 = (f32[2304,128]{1,0:T(8,128)S(1)}, f32[1152,128]{1,0:T(8,128)S(1)}) custom-call(bf16[64,2,2304]{2,1,0:T(2,128)(2,1)S(1)} %bitcast.9, bf16[1,2304]{1,0:T(2,128)(2,1)S(1)} %copy-done.1, bf16[128,128]{1,0:T(8,128)(2,1)S(1)} %make_eye.1.eye_ref), custom_call_target="tpu_custom_call" | custom-call | tf_op jit(solution)/shard_map/turn_orbitals/pallas_call | solution.py:219
  5.6 0.1 collective-permute-done.far_ref
  5.6 3.1 %filter_box.1 = (bf16[128,2304]{1,0:T(8,128)(2,1)S(1)}, f32[2,2304]{1,0:T(2,128)S(1)}) custom-call(s32[1,8]{1,0:T(1,128)} %counts_hbm.1, s32[1,1]{1,0:T(1,128)S(6)} %copy.9.parity_any, f32[2304,128]{1,0:T(8,128)S(1)} %get-tuple-element.6.plain, f32[1152,128]{1,0:T(8,128)S(1)} %get-tuple-element.7.near_diagonal, bf16[1,2304]{1,0:T(2,128)(2,1)S(1)} %collective-permute-done.far_ref), custom_call_target="tpu_custom_call" | custom-call | tf_op jit(solution)/shard_map/filter_box/pallas_call | solution.py:237
  8.7 2.7 %collective-permute-start.1 = (f32[2,1152]{1,0:T(2,128)S(1)}, f32[2,1152]{1,0:T(2,128)S(1)}, u32[]{:S(2)}, u32[]{:S(2)}) collective-permute-start(f32[2,1152]{1,0:T(2,128)S(1)} %broadcast_select_fusion), channel_id=1, source_target_pairs={{0,16},{8,24},{16,0},{24,8},{1,17},{9,25},{17,1},{25,9},{2,18},{10... | collective-permute-start | bytes 27656 | tf_op jit(solution)/shard_map/ppermute | solution.py:264
  11.4 2.0 %collective-permute-done.1 = f32[2,1152]{1,0:T(2,128)S(1)} collective-permute-done((f32[2,1152]{1,0:T(2,128)S(1)}, f32[2,1152]{1,0:T(2,128)S(1)}, u32[]{:S(2)}, u32[]{:S(2)}) %collective-permute-start.1) | collective-permute-done | bytes 9248 | tf_op jit(solution)/shard_map/ppermute | solution.py:264
  13.4 0.1 broadcast_select_fusion.1
  13.5 1.6 %collective-permute-start.2 = (f32[2,576]{1,0:T(2,128)S(1)}, f32[2,576]{1,0:T(2,128)S(1)}, u32[]{:S(2)}, u32[]{:S(2)}) collective-permute-start(f32[2,576]{1,0:T(2,128)S(1)} %broadcast_select_fusion.1), channel_id=1, source_target_pairs={{0,8},{8,0},{16,24},{24,16},{1,9},{9,1},{17,25},{25,17},{2,10},{10... | collective-permute-start | bytes 13832 | tf_op jit(solution)/shard_map/ppermute | solution.py:264
  15.0 2.0 %collective-permute-done.2 = f32[2,576]{1,0:T(2,128)S(1)} collective-permute-done((f32[2,576]{1,0:T(2,128)S(1)}, f32[2,576]{1,0:T(2,128)S(1)}, u32[]{:S(2)}, u32[]{:S(2)}) %collective-permute-start.2) | collective-permute-done | bytes 4640 | tf_op jit(solution)/shard_map/ppermute | solution.py:264
  17.1 0.1 select_add_fusion.1
  17.2 0.1 collective-permute-start.3
  17.2 1.4 %copy.8 = bf16[2,64,2304]{2,0,1:T(2,128)(2,1)} copy(bf16[2,64,2304]{2,1,0:T(8,128)(2,1)S(1)} %bitcast.10) | data formatting | bytes 1179648 | tf_op jit(solution)/shard_map/reshape | solution.py:279
  18.7 2.5 %collective-permute-done.3 = f32[1,576]{1,0:T(1,128)S(1)} collective-permute-done((f32[1,576]{1,0:T(1,128)S(1)}, f32[1,576]{1,0:T(1,128)S(1)}, u32[]{:S(2)}, u32[]{:S(2)}) %collective-permute-start.3) | collective-permute-done | bytes 2336 | tf_op jit(solution)/shard_map/ppermute | solution.py:278
  21.1 0.6 %fusion = f32[1,1,576]{2,1,0:T(1,128)} fusion(f32[1,576]{1,0:T(1,128)S(1)} %collective-permute-done.3, f32[2,576]{1,0:T(2,128)S(1)} %select_add_fusion.1), kind=kLoop, calls=%fused_computation.6 | loop fusion | flops 576 | bytes 6912 | tf_op jit(solution)/shard_map/broadcast_in_dim | solution.py:280
  (4 shorter events, 0.0 us)
Async XLA Ops:
  0.6 4.1 %copy-start.1 = (bf16[1,2304]{1,0:T(2,128)(2,1)S(1)}, bf16[1,2304]{1,0:T(2,128)(2,1)}, u32[]{:S(2)}) copy-start(bf16[1,2304]{1,0:T(2,128)(2,1)} %near_ref.1) | copy-start | bytes 13828
  0.6 4.1 %copy-start = (bf16[1,1,64,2,2304]{4,3,2,1,0:T(2,128)(2,1)S(1)}, bf16[1,1,64,2,2304]{4,3,2,1,0:T(2,128)(2,1)}, u32[]{:S(2)}) copy-start(bf16[1,1,64,2,2304]{4,3,2,1,0:T(2,128)(2,1)} %param.4) | copy-start | bytes 1769476
  0.6 5.0 %collective-permute-start = (bf16[1,2304]{1,0:T(2,128)(2,1)}, bf16[1,2304]{1,0:T(2,128)(2,1)S(1)}, u32[]{:S(2)}, u32[]{:S(2)}) collective-permute-start(bf16[1,2304]{1,0:T(2,128)(2,1)} %near_ref.1), channel_id=1, source_target_pairs={{1,0},{2,1},{3,2},{4,3},{5,4},{6,5},{7,6},{0,7},{9,8},{10,9},{11,1... | collective-permute-start | bytes 13832 | tf_op jit(solution)/shard_map/ppermute | solution.py:272
  8.7 4.6 %collective-permute-start.1 = (f32[2,1152]{1,0:T(2,128)S(1)}, f32[2,1152]{1,0:T(2,128)S(1)}, u32[]{:S(2)}, u32[]{:S(2)}) collective-permute-start(f32[2,1152]{1,0:T(2,128)S(1)} %broadcast_select_fusion), channel_id=1, source_target_pairs={{0,16},{8,24},{16,0},{24,8},{1,17},{9,25},{17,1},{25,9},{2,18},{10... | collective-permute-start | bytes 27656 | tf_op jit(solution)/shard_map/ppermute | solution.py:264
  13.5 3.6 %collective-permute-start.2 = (f32[2,576]{1,0:T(2,128)S(1)}, f32[2,576]{1,0:T(2,128)S(1)}, u32[]{:S(2)}, u32[]{:S(2)}) collective-permute-start(f32[2,576]{1,0:T(2,128)S(1)} %broadcast_select_fusion.1), channel_id=1, source_target_pairs={{0,8},{8,0},{16,24},{24,16},{1,9},{9,1},{17,25},{25,17},{2,10},{10... | collective-permute-start | bytes 13832 | tf_op jit(solution)/shard_map/ppermute | solution.py:264
  17.2 4.0 %collective-permute-start.3 = (f32[1,576]{1,0:T(1,128)S(1)}, f32[1,576]{1,0:T(1,128)S(1)}, u32[]{:S(2)}, u32[]{:S(2)}) collective-permute-start(f32[1,576]{1,0:T(1,128)S(1)} %slice.31), channel_id=1, source_target_pairs={{0,1},{1,2},{2,3},{3,4},{4,5},{5,6},{6,7},{7,0},{8,9},{9,10},{10,1... | collective-permute-start | bytes 6920 | tf_op jit(solution)/shard_map/ppermute | solution.py:278

commit v5 on v4

--- a/solution.py
+++ b/solution.py
@@ -29,7 +29,7 @@
     return order
 
 
-SHIFTS = [filter_half * root for root in leja_roots()]
+SHIFTS = [filter_half * root + filter_centre - 6.0 for root in leja_roots()]
 LEADING = 2.0 ** (DEGREE - 1) / filter_half**DEGREE
 
 
@@ -63,37 +63,26 @@
         )
         plain[start : start + CHUNK, :] = turned[:, :rows]
         plain[half + start : half + start + CHUNK, :] = turned[:, rows : 2 * rows]
-        near_diagonal[start : start + CHUNK, :] = turned[:, 2 * rows :] + (6.0 - filter_centre)
+        near_diagonal[start : start + CHUNK, :] = turned[:, 2 * rows :]
 
 
 def filter_kernel(
-    counts_hbm,
-    parity_any,
+    marks_ref,
     plain,
     near_diagonal,
     far_ref,
     filtered_ref,
     halves_ref,
-    counts_ref,
-    parity_ref,
     ordered,
     far_diagonal,
     one,
     two,
     final,
-    sems,
 ):
     cells, rows = plain.shape
     slots, half = rows // 2, cells // 2
     strips = BZ // SUB
     height = half // BZ
-
-    small = [
-        pltpu.make_async_copy(counts_hbm, counts_ref, sems.at[0]),
-        pltpu.make_async_copy(parity_any, parity_ref, sems.at[1]),
-    ]
-    for copy in small:
-        copy.start()
 
     eye = identity(CHUNK)
     for start in range(0, half, CHUNK):
@@ -103,7 +92,7 @@
             across,
             preferred_element_type=jnp.float32,
         )
-        far_diagonal[start : start + CHUNK, :] = potential + (6.0 - filter_centre)
+        far_diagonal[start : start + CHUNK, :] = potential
 
     sub_ids = lax.broadcasted_iota(jnp.int32, (SUB, rows), 0)
     is_first, is_last = sub_ids == 0, sub_ids == SUB - 1
@@ -177,17 +166,18 @@
 
     sweep(functools.partial(packed, one), factor_last)
 
-    for copy in small:
-        copy.wait()
-    count = counts_ref[0, lax.axis_index("dev")]
-    signed = (1.0 - 2.0 * parity_ref[0, 0].astype(jnp.float32)) / slots
+    marks = marks_ref[...]
+    places = lax.broadcasted_iota(jnp.int32, marks.shape, 1)
+    count = jnp.sum(jnp.where(places == lax.axis_index("dev"), marks, 0), axis=1, keepdims=True)
+    parity = jnp.sum(jnp.where(places == marks.shape[1] - 1, marks, 0), axis=1, keepdims=True)
+    signed = (1.0 - 2.0 * parity.astype(jnp.float32)) / slots
 
     lane_sum = jnp.broadcast_to(jnp.sum(totals[0], axis=0, keepdims=True), (SUB, rows))
     mean_square = (lane_sum + pltpu.roll(lane_sum, slots, 1)) * (LEADING * LEADING / (2 * cells))
     slot_ids = lax.broadcasted_iota(jnp.int32, (SUB, rows), 1) % slots
     scale = jnp.where(slot_ids < count, LEADING * lax.rsqrt(mean_square + 1e-06), 0.0)[:1]
 
-    wide = 3 * CHUNK if half % (3 * CHUNK) == 0 else CHUNK
+    wide = 9 * CHUNK
     for x in range(2):
         for start in range(0, half, wide):
             at = x * half + start
@@ -229,53 +219,60 @@
     )(orbitals, near, eye)
 
 
-def filter_box(counts, parity, plain, near_diagonal, far):
+def filter_box(marks, plain, near_diagonal, far):
     cells, rows = plain.shape
     field, half = pltpu.VMEM((cells, rows), jnp.float32), pltpu.VMEM((cells // 2, rows), jnp.float32)
-    vmem, hbm = pl.BlockSpec(memory_space=pltpu.VMEM), pl.BlockSpec(memory_space=pltpu.HBM)
-    counts = pltpu.with_memory_space_constraint(counts, pltpu.HBM)
+    vmem = pl.BlockSpec(memory_space=pltpu.VMEM)
     return pl.pallas_call(
         filter_kernel,
         out_shape=(
             jax.ShapeDtypeStruct((rows, cells), jnp.bfloat16),
             jax.ShapeDtypeStruct((2, cells), jnp.float32),
         ),
-        in_specs=[hbm, pl.BlockSpec(memory_space=pl.ANY)] + [vmem] * 3,
+        in_specs=[vmem] * 4,
         out_specs=(vmem, vmem),
-        scratch_shapes=[pltpu.SMEM(counts.shape, jnp.int32), pltpu.SMEM(parity.shape, jnp.int32)]
-        + [field, half, field, field, field]
-        + [pltpu.SemaphoreType.DMA((2,))],
+        scratch_shapes=[field, half, field, field, field],
         compiler_params=pltpu.CompilerParams(vmem_limit_bytes=16 * 2**20),
         name="filter_box",
-    )(counts, parity, plain, near_diagonal, far)
-
-
-def sum_over(part, axis):
-    size = lax.axis_size(axis)
-    if size & (size - 1):
-        return lax.psum_scatter(part, axis, scatter_dimension=1, tiled=True)
-    me = lax.axis_index(axis)
-    span = size // 2
-    while span:
-        half = part.shape[1] // 2
-        is_low = (me & span) == 0
-        kept = jnp.where(is_low, part[:, :half], part[:, half:])
-        sent = jnp.where(is_low, part[:, half:], part[:, :half])
-        part = kept + lax.ppermute(sent, axis, [(i, i ^ span) for i in range(size)])
+    )(marks, plain, near_diagonal, far)
+
+
+def by_halves(part, span):
+    half = part.shape[1] // 2
+    is_low = (lax.axis_index("grp") & span) == 0
+    low, high = part[:, :half], part[:, half:]
+    return jnp.where(is_low, low, high), jnp.where(is_low, high, low)
+
+
+def sum_blocks(halves):
+    groups, devs = lax.axis_size("grp"), lax.axis_size("dev")
+    onward = [(d, (d + 1) % devs) for d in range(devs)]
+    if groups & (groups - 1) or groups == 1:
+        sums = lax.psum_scatter(halves, "grp", scatter_dimension=1, tiled=True)
+        return sums[:1] + lax.ppermute(sums[1:], "dev", onward)
+    span = groups // 2
+    while span > 1:
+        mine, other = by_halves(halves, span)
+        halves = mine + lax.ppermute(other, "grp", [(g, g ^ span) for g in range(groups)])
         span //= 2
-    return part
+    mine, other = by_halves(halves, 1)
+    both_axes = ("grp", "dev")
+    places = [(g, d) for g in range(groups) for d in range(devs)]
+    carried = lax.ppermute(mine[1:], both_axes, [(g * devs + d, g * devs + (d + 1) % devs) for g, d in places])
+    beside = lax.ppermute(other[:1], both_axes, [(g * devs + d, (g ^ 1) * devs + d) for g, d in places])
+    slanted = lax.ppermute(other[1:], both_axes, [(g * devs + d, (g ^ 1) * devs + (d + 1) % devs) for g, d in places])
+    return mine[:1] + carried + beside + slanted
 
 
 def on_device(orbitals, potential, counts, parity):
     group_size = lax.axis_size("dev")
     slots, _, cells = orbitals.shape[2:]
     far = lax.ppermute(potential, "dev", [((i + 1) % group_size, i) for i in range(group_size)])
+    marks = jnp.concatenate([counts, parity], 1)
     eye = make_eye()
     plain, near_diagonal = turn_orbitals(orbitals[0, 0], potential, eye)
-    filtered_rows, halves = filter_box(counts, parity, plain, near_diagonal, far)
-    halves = sum_over(halves, "grp")
-    onward = [(i, (i + 1) % group_size) for i in range(group_size)]
-    density = halves[:1] + lax.ppermute(halves[1:], "dev", onward)
+    filtered_rows, halves = filter_box(marks, plain, near_diagonal, far)
+    density = sum_blocks(halves)
     filtered = jnp.swapaxes(filtered_rows.reshape(2, slots, cells), 0, 1)
     return density[None], filtered[None, None]
 

time: 21.9 us -> 20.6 us (0.941)
  waiting for transfers between devices: 6.56 us -> 5.31 us
    ppermute x3 -> x4, waiting for transfers between devices: 6.49 us -> 5.29 us  [the longest x1 2.8 us: sum_blocks(): lax.ppermute(other[1:], both_axes, [(g * devs + d, (g ^ 1) * devs + (d +...]
    ppermute x3 -> x4, starting transfers between devices: 4.3 us -> 4.36 us  [the longest x1 2.65 us: sum_blocks(): lax.ppermute(other, 'grp', [(g, g ^ span) for g in range(groups)])]
  transfers between devices with their start and end apart: 4 -> 5, of which waited for: 4 -> 3; matrix products, arithmetic and copies ran while one was open for 7% -> 7% of each run, Pallas kernels for 4% -> 4%
where the time goes in v5:
time: 20.6 us; the launch traced here: 20.4 us
  starting transfers between devices  7.74 us (38%)
  waiting for transfers between devices  5.31 us (26%)
  Pallas kernels  3.82 us (19%)
  local copies, waits for them, and re-layouts  1.45 us (7%)
  between operations  1.36 us (7%)
  other arithmetic  0.75 us (4%)
    ppermute x1, starting transfers between devices, on_device(): lax.ppermute(potential, 'dev', [((i + 1) % group_size, i) for i in range(...  3.39 us
    pallas_call x1, Pallas kernels, filter_box(): pl.pallas_call(filter_kernel, out_shape=(jax.ShapeDtypeStruct((rows, cell...  3.01 us
    ppermute x1, waiting for transfers between devices, sum_blocks(): lax.ppermute(other[1:], both_axes, [(g * devs + d, (g ^ 1) * devs + (d +...  2.8 us
    ppermute x1, starting transfers between devices, sum_blocks(): lax.ppermute(other, 'grp', [(g, g ^ span) for g in range(groups)])  2.65 us
    ppermute x1, waiting for transfers between devices, sum_blocks(): lax.ppermute(other, 'grp', [(g, g ^ span) for g in range(groups)])  1.97 us
    ppermute x1, starting transfers between devices, sum_blocks(): lax.ppermute(other[:1], both_axes, [(g * devs + d, (g ^ 1) * devs + d) fo...  1.64 us
    reshape x1, local copies, waits for them, and re-layouts, on_device(): filtered = jnp.swapaxes(filtered_rows.reshape(2, slots, cells), 0, 1)  1.42 us
    pallas_call x1, Pallas kernels, turn_orbitals(): pl.pallas_call(turn_kernel, out_shape=(jax.ShapeDtypeStruct((cells, plane...  0.8 us
  transfers between devices with their start and end apart: 5, of which 3 were waited for; matrix products, arithmetic and copies ran while one was open for 7% of the time, Pallas kernels for 4%

profile of v5, /device:TPU:0, one launch (start us, length us, event | category | flops | bytes accessed | tf_op | source)
XLA Modules:
  0.0 20.4 jit_solution(13729621883705061149)
XLA Ops:
  0.6 0.0 copy-start.1
  0.6 0.0 copy-start.2
  0.6 0.0 copy-start
  0.7 3.4 %collective-permute-start = (bf16[1,2304]{1,0:T(2,128)(2,1)}, bf16[1,2304]{1,0:T(2,128)(2,1)S(1)}, u32[]{:S(2)}, u32[]{:S(2)}) collective-permute-start(bf16[1,2304]{1,0:T(2,128)(2,1)} %near_ref.1), channel_id=1, source_target_pairs={{1,0},{2,1},{3,2},{4,3},{5,4},{6,5},{7,6},{0,7},{9,8},{10,9},{11,1... | collective-permute-start | bytes 13832 | tf_op jit(solution)/shard_map/ppermute | solution.py:270
  4.7 0.0 copy-done.2
  4.7 0.1 pad_add_fusion.marks_ref
  4.8 0.0 copy-done.1
  4.8 0.0 copy-done
  4.8 0.8 %turn_orbitals.1 = (f32[2304,128]{1,0:T(8,128)S(1)}, f32[1152,128]{1,0:T(8,128)S(1)}) custom-call(bf16[64,2,2304]{2,1,0:T(2,128)(2,1)S(1)} %bitcast.9, bf16[1,2304]{1,0:T(2,128)(2,1)S(1)} %copy-done.1, bf16[128,128]{1,0:T(8,128)(2,1)S(1)} %make_eye.1.eye_ref), custom_call_target="tpu_custom_call" | custom-call | tf_op jit(solution)/shard_map/turn_orbitals/pallas_call | solution.py:209
  5.6 0.0 collective-permute-done.far_ref
  5.6 3.0 %filter_box.1 = (bf16[128,2304]{1,0:T(8,128)(2,1)S(1)}, f32[2,2304]{1,0:T(2,128)S(1)}) custom-call(s32[1,9]{1,0:T(1,128)S(1)} %pad_add_fusion.marks_ref, f32[2304,128]{1,0:T(8,128)S(1)} %get-tuple-element.6.plain, f32[1152,128]{1,0:T(8,128)S(1)} %get-tuple-element.7.near_diagonal, bf16[1,2304]{1,0:T(2,128)(2,1)S(1)} %collective-permute-done.far_ref), custom_call_target="tpu_custom_call" | custom-call | tf_op jit(solution)/shard_map/filter_box/pallas_call | solution.py:226
  8.7 2.7 %collective-permute-start.1 = (f32[2,1152]{1,0:T(2,128)S(1)}, f32[2,1152]{1,0:T(2,128)S(1)}, u32[]{:S(2)}, u32[]{:S(2)}) collective-permute-start(f32[2,1152]{1,0:T(2,128)S(1)} %broadcast_select_fusion), channel_id=1, source_target_pairs={{0,16},{8,24},{16,0},{24,8},{1,17},{9,25},{17,1},{25,9},{2,18},{10... | collective-permute-start | bytes 27656 | tf_op jit(solution)/shard_map/ppermute | solution.py:256
  11.3 2.0 %collective-permute-done.1 = f32[2,1152]{1,0:T(2,128)S(1)} collective-permute-done((f32[2,1152]{1,0:T(2,128)S(1)}, f32[2,1152]{1,0:T(2,128)S(1)}, u32[]{:S(2)}, u32[]{:S(2)}) %collective-permute-start.1) | collective-permute-done | bytes 9248 | tf_op jit(solution)/shard_map/ppermute | solution.py:256
  13.3 0.1 broadcast_select_fusion.2
  13.4 1.6 %collective-permute-start.3 = (f32[1,576]{1,0:T(1,128)S(1)}, f32[1,576]{1,0:T(1,128)S(1)}, u32[]{:S(2)}, u32[]{:S(2)}) collective-permute-start(f32[1,576]{1,0:T(1,128)S(1)} %get-tuple-element.12), channel_id=1, source_target_pairs={{0,8},{1,9},{2,10},{3,11},{4,12},{5,13},{6,14},{7,15},{8,0},{9,1},... | collective-permute-start | bytes 6920 | tf_op jit(solution)/shard_map/ppermute | solution.py:262
  15.0 0.0 collective-permute-start.4
  15.0 0.1 collective-permute-start.2
  15.1 1.4 %copy.8 = bf16[2,64,2304]{2,0,1:T(2,128)(2,1)} copy(bf16[2,64,2304]{2,1,0:T(8,128)(2,1)S(1)} %bitcast.10) | data formatting | bytes 1179648 | tf_op jit(solution)/shard_map/reshape | solution.py:276
  16.5 0.5 %collective-permute-done.3 = f32[1,576]{1,0:T(1,128)S(1)} collective-permute-done((f32[1,576]{1,0:T(1,128)S(1)}, f32[1,576]{1,0:T(1,128)S(1)}, u32[]{:S(2)}, u32[]{:S(2)}) %collective-permute-start.3) | collective-permute-done | bytes 2336 | tf_op jit(solution)/shard_map/ppermute | solution.py:262
  17.0 2.8 %collective-permute-done.4 = f32[1,576]{1,0:T(1,128)S(1)} collective-permute-done((f32[1,576]{1,0:T(1,128)S(1)}, f32[1,576]{1,0:T(1,128)S(1)}, u32[]{:S(2)}, u32[]{:S(2)}) %collective-permute-start.4) | collective-permute-done | bytes 2336 | tf_op jit(solution)/shard_map/ppermute | solution.py:263
  19.8 0.0 collective-permute-done.2
  19.8 0.6 %fusion.2 = f32[1,1,576]{2,1,0:T(1,128)} fusion(f32[1,576]{1,0:T(1,128)S(1)} %collective-permute-done.4, f32[1,576]{1,0:T(1,128)S(1)} %collective-permute-done.3, f32[1,576]{1,0:T(1,128)S(1)} %collective-permute-done.2, f32[2,576]{1,0:T(2,128)S(1)} %get-tuple-element.10), kind=kLoop, calls=%fused_computation.8 | loop fusion | flops 1728 | bytes 11520 | tf_op jit(solution)/shard_map/broadcast_in_dim | solution.py:277
  (5 shorter events, 0.0 us)
Async XLA Ops:
  0.6 4.2 %copy-start.1 = (bf16[1,2304]{1,0:T(2,128)(2,1)S(1)}, bf16[1,2304]{1,0:T(2,128)(2,1)}, u32[]{:S(2)}) copy-start(bf16[1,2304]{1,0:T(2,128)(2,1)} %near_ref.1) | copy-start | bytes 13828
  0.6 4.1 %copy-start.2 = (s32[1,8]{1,0:T(1,128)S(1)}, s32[1,8]{1,0:T(1,128)}, u32[]{:S(2)}) copy-start(s32[1,8]{1,0:T(1,128)} %param.6) | copy-start | bytes 100
  0.6 4.2 %copy-start = (bf16[1,1,64,2,2304]{4,3,2,1,0:T(2,128)(2,1)S(1)}, bf16[1,1,64,2,2304]{4,3,2,1,0:T(2,128)(2,1)}, u32[]{:S(2)}) copy-start(bf16[1,1,64,2,2304]{4,3,2,1,0:T(2,128)(2,1)} %param.4) | copy-start | bytes 1769476
  0.7 5.0 %collective-permute-start = (bf16[1,2304]{1,0:T(2,128)(2,1)}, bf16[1,2304]{1,0:T(2,128)(2,1)S(1)}, u32[]{:S(2)}, u32[]{:S(2)}) collective-permute-start(bf16[1,2304]{1,0:T(2,128)(2,1)} %near_ref.1), channel_id=1, source_target_pairs={{1,0},{2,1},{3,2},{4,3},{5,4},{6,5},{7,6},{0,7},{9,8},{10,9},{11,1... | collective-permute-start | bytes 13832 | tf_op jit(solution)/shard_map/ppermute | solution.py:270
  8.7 4.6 %collective-permute-start.1 = (f32[2,1152]{1,0:T(2,128)S(1)}, f32[2,1152]{1,0:T(2,128)S(1)}, u32[]{:S(2)}, u32[]{:S(2)}) collective-permute-start(f32[2,1152]{1,0:T(2,128)S(1)} %broadcast_select_fusion), channel_id=1, source_target_pairs={{0,16},{8,24},{16,0},{24,8},{1,17},{9,25},{17,1},{25,9},{2,18},{10... | collective-permute-start | bytes 27656 | tf_op jit(solution)/shard_map/ppermute | solution.py:256
  13.4 3.7 %collective-permute-start.3 = (f32[1,576]{1,0:T(1,128)S(1)}, f32[1,576]{1,0:T(1,128)S(1)}, u32[]{:S(2)}, u32[]{:S(2)}) collective-permute-start(f32[1,576]{1,0:T(1,128)S(1)} %get-tuple-element.12), channel_id=1, source_target_pairs={{0,8},{1,9},{2,10},{3,11},{4,12},{5,13},{6,14},{7,15},{8,0},{9,1},... | collective-permute-start | bytes 6920 | tf_op jit(solution)/shard_map/ppermute | solution.py:262
  15.0 4.8 %collective-permute-start.4 = (f32[1,576]{1,0:T(1,128)S(1)}, f32[1,576]{1,0:T(1,128)S(1)}, u32[]{:S(2)}, u32[]{:S(2)}) collective-permute-start(f32[1,576]{1,0:T(1,128)S(1)} %get-tuple-element.13), channel_id=1, source_target_pairs={{0,9},{1,10},{2,11},{3,12},{4,13},{5,14},{6,15},{7,8},{8,1},{9,2},... | collective-permute-start | bytes 6920 | tf_op jit(solution)/shard_map/ppermute | solution.py:263
  15.0 4.8 %collective-permute-start.2 = (f32[1,576]{1,0:T(1,128)S(1)}, f32[1,576]{1,0:T(1,128)S(1)}, u32[]{:S(2)}, u32[]{:S(2)}) collective-permute-start(f32[1,576]{1,0:T(1,128)S(1)} %slice.35), channel_id=1, source_target_pairs={{0,1},{1,2},{2,3},{3,4},{4,5},{5,6},{6,7},{7,0},{8,9},{9,10},{10,1... | collective-permute-start | bytes 6920 | tf_op jit(solution)/shard_map/ppermute | solution.py:261

commit v6 on v5

--- a/solution.py
+++ b/solution.py
@@ -261,7 +261,7 @@
     carried = lax.ppermute(mine[1:], both_axes, [(g * devs + d, g * devs + (d + 1) % devs) for g, d in places])
     beside = lax.ppermute(other[:1], both_axes, [(g * devs + d, (g ^ 1) * devs + d) for g, d in places])
     slanted = lax.ppermute(other[1:], both_axes, [(g * devs + d, (g ^ 1) * devs + (d + 1) % devs) for g, d in places])
-    return mine[:1] + carried + beside + slanted
+    return mine[:1] + carried + slanted + beside
 
 
 def on_device(orbitals, potential, counts, parity):

time: 20.6 us -> 19.8 us (0.961)
  waiting for transfers between devices: 5.31 us -> 4.48 us
    ppermute x1, waiting for transfers between devices: 2.8 us -> 1.72 us  [sum_blocks(): lax.ppermute(other[1:], both_axes, [(g * devs + d, (g ^ 1) * devs + (d +...]
    ppermute x1, waiting for transfers between devices: 0.01 us -> 0.76 us  [sum_blocks(): lax.ppermute(mine[1:], both_axes, [(g * devs + d, g * devs + (d + 1) % de...]
    ppermute x1, waiting for transfers between devices: 0.51 us -> 0.01 us  [sum_blocks(): lax.ppermute(other[:1], both_axes, [(g * devs + d, (g ^ 1) * devs + d) fo...]
  transfers between devices with their start and end apart: 5 -> 5, of which waited for: 3 -> 3; matrix products, arithmetic and copies ran while one was open for 7% -> 8% of each run, Pallas kernels for 4% -> 4%
where the time goes in v6:
time: 19.8 us; the launch traced here: 19.6 us
  starting transfers between devices  7.74 us (39%)
  waiting for transfers between devices  4.48 us (23%)
  Pallas kernels  3.82 us (19%)
  local copies, waits for them, and re-layouts  1.45 us (7%)
  between operations  1.36 us (7%)
  other arithmetic  0.75 us (4%)
    ppermute x1, starting transfers between devices, on_device(): lax.ppermute(potential, 'dev', [((i + 1) % group_size, i) for i in range(...  3.39 us
    pallas_call x1, Pallas kernels, filter_box(): pl.pallas_call(filter_kernel, out_shape=(jax.ShapeDtypeStruct((rows, cell...  3.01 us
    ppermute x1, starting transfers between devices, sum_blocks(): lax.ppermute(other, 'grp', [(g, g ^ span) for g in range(groups)])  2.65 us
    ppermute x1, waiting for transfers between devices, sum_blocks(): lax.ppermute(other, 'grp', [(g, g ^ span) for g in range(groups)])  1.97 us
    ppermute x1, waiting for transfers between devices, sum_blocks(): lax.ppermute(other[1:], both_axes, [(g * devs + d, (g ^ 1) * devs + (d +...  1.72 us
    ppermute x1, starting transfers between devices, sum_blocks(): lax.ppermute(other[:1], both_axes, [(g * devs + d, (g ^ 1) * devs + d) fo...  1.64 us
    reshape x1, local copies, waits for them, and re-layouts, on_device(): filtered = jnp.swapaxes(filtered_rows.reshape(2, slots, cells), 0, 1)  1.42 us
    pallas_call x1, Pallas kernels, turn_orbitals(): pl.pallas_call(turn_kernel, out_shape=(jax.ShapeDtypeStruct((cells, plane...  0.8 us
  transfers between devices with their start and end apart: 5, of which 3 were waited for; matrix products, arithmetic and copies ran while one was open for 8% of the time, Pallas kernels for 4%

profile of v6, /device:TPU:0, one launch (start us, length us, event | category | flops | bytes accessed | tf_op | source)
XLA Modules:
  0.0 19.6 jit_solution(3913338949735543112)
XLA Ops:
  0.6 0.0 copy-start.1
  0.6 0.0 copy-start.2
  0.6 0.0 copy-start
  0.7 3.4 %collective-permute-start = (bf16[1,2304]{1,0:T(2,128)(2,1)}, bf16[1,2304]{1,0:T(2,128)(2,1)S(1)}, u32[]{:S(2)}, u32[]{:S(2)}) collective-permute-start(bf16[1,2304]{1,0:T(2,128)(2,1)} %near_ref.1), channel_id=1, source_target_pairs={{1,0},{2,1},{3,2},{4,3},{5,4},{6,5},{7,6},{0,7},{9,8},{10,9},{11,1... | collective-permute-start | bytes 13832 | tf_op jit(solution)/shard_map/ppermute | solution.py:270
  4.7 0.0 copy-done.2
  4.7 0.1 pad_add_fusion.marks_ref
  4.8 0.0 copy-done.1
  4.8 0.0 copy-done
  4.8 0.8 %turn_orbitals.1 = (f32[2304,128]{1,0:T(8,128)S(1)}, f32[1152,128]{1,0:T(8,128)S(1)}) custom-call(bf16[64,2,2304]{2,1,0:T(2,128)(2,1)S(1)} %bitcast.9, bf16[1,2304]{1,0:T(2,128)(2,1)S(1)} %copy-done.1, bf16[128,128]{1,0:T(8,128)(2,1)S(1)} %make_eye.1.eye_ref), custom_call_target="tpu_custom_call" | custom-call | tf_op jit(solution)/shard_map/turn_orbitals/pallas_call | solution.py:209
  5.6 0.0 collective-permute-done.far_ref
  5.6 3.0 %filter_box.1 = (bf16[128,2304]{1,0:T(8,128)(2,1)S(1)}, f32[2,2304]{1,0:T(2,128)S(1)}) custom-call(s32[1,9]{1,0:T(1,128)S(1)} %pad_add_fusion.marks_ref, f32[2304,128]{1,0:T(8,128)S(1)} %get-tuple-element.6.plain, f32[1152,128]{1,0:T(8,128)S(1)} %get-tuple-element.7.near_diagonal, bf16[1,2304]{1,0:T(2,128)(2,1)S(1)} %collective-permute-done.far_ref), custom_call_target="tpu_custom_call" | custom-call | tf_op jit(solution)/shard_map/filter_box/pallas_call | solution.py:226
  8.7 2.7 %collective-permute-start.1 = (f32[2,1152]{1,0:T(2,128)S(1)}, f32[2,1152]{1,0:T(2,128)S(1)}, u32[]{:S(2)}, u32[]{:S(2)}) collective-permute-start(f32[2,1152]{1,0:T(2,128)S(1)} %broadcast_select_fusion), channel_id=1, source_target_pairs={{0,16},{8,24},{16,0},{24,8},{1,17},{9,25},{17,1},{25,9},{2,18},{10... | collective-permute-start | bytes 27656 | tf_op jit(solution)/shard_map/ppermute | solution.py:256
  11.3 2.0 %collective-permute-done.1 = f32[2,1152]{1,0:T(2,128)S(1)} collective-permute-done((f32[2,1152]{1,0:T(2,128)S(1)}, f32[2,1152]{1,0:T(2,128)S(1)}, u32[]{:S(2)}, u32[]{:S(2)}) %collective-permute-start.1) | collective-permute-done | bytes 9248 | tf_op jit(solution)/shard_map/ppermute | solution.py:256
  13.3 0.1 broadcast_select_fusion.2
  13.4 0.1 collective-permute-start.3
  13.5 1.6 %collective-permute-start.4 = (f32[1,576]{1,0:T(1,128)S(1)}, f32[1,576]{1,0:T(1,128)S(1)}, u32[]{:S(2)}, u32[]{:S(2)}) collective-permute-start(f32[1,576]{1,0:T(1,128)S(1)} %get-tuple-element.13), channel_id=1, source_target_pairs={{0,8},{1,9},{2,10},{3,11},{4,12},{5,13},{6,14},{7,15},{8,0},{9,1},... | collective-permute-start | bytes 6920 | tf_op jit(solution)/shard_map/ppermute | solution.py:262
  15.1 0.0 collective-permute-start.2
  15.1 1.4 %copy.8 = bf16[2,64,2304]{2,0,1:T(2,128)(2,1)} copy(bf16[2,64,2304]{2,1,0:T(8,128)(2,1)S(1)} %bitcast.10) | data formatting | bytes 1179648 | tf_op jit(solution)/shard_map/reshape | solution.py:276
  16.5 1.7 %collective-permute-done.3 = f32[1,576]{1,0:T(1,128)S(1)} collective-permute-done((f32[1,576]{1,0:T(1,128)S(1)}, f32[1,576]{1,0:T(1,128)S(1)}, u32[]{:S(2)}, u32[]{:S(2)}) %collective-permute-start.3) | collective-permute-done | bytes 2336 | tf_op jit(solution)/shard_map/ppermute | solution.py:263
  18.3 0.0 collective-permute-done.4
  18.3 0.8 %collective-permute-done.2 = f32[1,576]{1,0:T(1,128)S(1)} collective-permute-done((f32[1,576]{1,0:T(1,128)S(1)}, f32[1,576]{1,0:T(1,128)S(1)}, u32[]{:S(2)}, u32[]{:S(2)}) %collective-permute-start.2) | collective-permute-done | bytes 2336 | tf_op jit(solution)/shard_map/ppermute | solution.py:261
  19.0 0.6 %fusion.2 = f32[1,1,576]{2,1,0:T(1,128)} fusion(f32[1,576]{1,0:T(1,128)S(1)} %collective-permute-done.4, f32[1,576]{1,0:T(1,128)S(1)} %collective-permute-done.3, f32[1,576]{1,0:T(1,128)S(1)} %collective-permute-done.2, f32[2,576]{1,0:T(2,128)S(1)} %get-tuple-element.10), kind=kLoop, calls=%fused_computation.8 | loop fusion | flops 1728 | bytes 11520 | tf_op jit(solution)/shard_map/broadcast_in_dim | solution.py:277
  (5 shorter events, 0.0 us)
Async XLA Ops:
  0.6 4.2 %copy-start.1 = (bf16[1,2304]{1,0:T(2,128)(2,1)S(1)}, bf16[1,2304]{1,0:T(2,128)(2,1)}, u32[]{:S(2)}) copy-start(bf16[1,2304]{1,0:T(2,128)(2,1)} %near_ref.1) | copy-start | bytes 13828
  0.6 4.1 %copy-start.2 = (s32[1,8]{1,0:T(1,128)S(1)}, s32[1,8]{1,0:T(1,128)}, u32[]{:S(2)}) copy-start(s32[1,8]{1,0:T(1,128)} %param.6) | copy-start | bytes 100
  0.6 4.2 %copy-start = (bf16[1,1,64,2,2304]{4,3,2,1,0:T(2,128)(2,1)S(1)}, bf16[1,1,64,2,2304]{4,3,2,1,0:T(2,128)(2,1)}, u32[]{:S(2)}) copy-start(bf16[1,1,64,2,2304]{4,3,2,1,0:T(2,128)(2,1)} %param.4) | copy-start | bytes 1769476
  0.7 5.0 %collective-permute-start = (bf16[1,2304]{1,0:T(2,128)(2,1)}, bf16[1,2304]{1,0:T(2,128)(2,1)S(1)}, u32[]{:S(2)}, u32[]{:S(2)}) collective-permute-start(bf16[1,2304]{1,0:T(2,128)(2,1)} %near_ref.1), channel_id=1, source_target_pairs={{1,0},{2,1},{3,2},{4,3},{5,4},{6,5},{7,6},{0,7},{9,8},{10,9},{11,1... | collective-permute-start | bytes 13832 | tf_op jit(solution)/shard_map/ppermute | solution.py:270
  8.7 4.6 %collective-permute-start.1 = (f32[2,1152]{1,0:T(2,128)S(1)}, f32[2,1152]{1,0:T(2,128)S(1)}, u32[]{:S(2)}, u32[]{:S(2)}) collective-permute-start(f32[2,1152]{1,0:T(2,128)S(1)} %broadcast_select_fusion), channel_id=1, source_target_pairs={{0,16},{8,24},{16,0},{24,8},{1,17},{9,25},{17,1},{25,9},{2,18},{10... | collective-permute-start | bytes 27656 | tf_op jit(solution)/shard_map/ppermute | solution.py:256
  13.4 4.9 %collective-permute-start.3 = (f32[1,576]{1,0:T(1,128)S(1)}, f32[1,576]{1,0:T(1,128)S(1)}, u32[]{:S(2)}, u32[]{:S(2)}) collective-permute-start(f32[1,576]{1,0:T(1,128)S(1)} %get-tuple-element.12), channel_id=1, source_target_pairs={{0,9},{1,10},{2,11},{3,12},{4,13},{5,14},{6,15},{7,8},{8,1},{9,2},... | collective-permute-start | bytes 6920 | tf_op jit(solution)/shard_map/ppermute | solution.py:263
  13.5 4.8 %collective-permute-start.4 = (f32[1,576]{1,0:T(1,128)S(1)}, f32[1,576]{1,0:T(1,128)S(1)}, u32[]{:S(2)}, u32[]{:S(2)}) collective-permute-start(f32[1,576]{1,0:T(1,128)S(1)} %get-tuple-element.13), channel_id=1, source_target_pairs={{0,8},{1,9},{2,10},{3,11},{4,12},{5,13},{6,14},{7,15},{8,0},{9,1},... | collective-permute-start | bytes 6920 | tf_op jit(solution)/shard_map/ppermute | solution.py:262
  15.1 3.9 %collective-permute-start.2 = (f32[1,576]{1,0:T(1,128)S(1)}, f32[1,576]{1,0:T(1,128)S(1)}, u32[]{:S(2)}, u32[]{:S(2)}) collective-permute-start(f32[1,576]{1,0:T(1,128)S(1)} %slice.35), channel_id=1, source_target_pairs={{0,1},{1,2},{2,3},{3,4},{4,5},{5,6},{6,7},{7,0},{8,9},{9,10},{10,1... | collective-permute-start | bytes 6920 | tf_op jit(solution)/shard_map/ppermute | solution.py:261

commit v7 on v6

--- a/solution.py
+++ b/solution.py
@@ -72,6 +72,8 @@
     near_diagonal,
     far_ref,
     filtered_ref,
+    kept_ref,
+    sent_ref,
     halves_ref,
     ordered,
     far_diagonal,
@@ -191,6 +193,22 @@
                 filtered_ref[x * slots : (x + 1) * slots, to] = rounded[mine]
                 halves_ref[x : x + 1, to] = jnp.sum(squares[mine], axis=0, keepdims=True) * signed
 
+    groups = lax.axis_size("grp")
+    me = lax.axis_index("grp")
+    width = cells // groups
+    room = kept_ref.shape[1] // (groups // 2)
+    parts = [halves_ref[:, i * width : (i + 1) * width] for i in range(groups)]
+    span = 1
+    while span < groups:
+        swapped = (me & span) != 0
+        parts = [jnp.where(swapped, parts[j ^ span], parts[j]) for j in range(groups)]
+        span *= 2
+    kept_ref[...] = jnp.zeros(kept_ref.shape, jnp.float32)
+    sent_ref[...] = jnp.zeros(sent_ref.shape, jnp.float32)
+    for j in range(groups // 2):
+        kept_ref[:, j * room : j * room + width] = parts[j]
+        sent_ref[:, j * room : j * room + width] = parts[groups // 2 + j]
+
 
 def make_eye():
     return pl.pallas_call(
@@ -223,45 +241,38 @@
     cells, rows = plain.shape
     field, half = pltpu.VMEM((cells, rows), jnp.float32), pltpu.VMEM((cells // 2, rows), jnp.float32)
     vmem = pl.BlockSpec(memory_space=pltpu.VMEM)
+    groups = lax.axis_size("grp")
+    room = pl.cdiv(cells // groups, 128) * 128
+    part = jax.ShapeDtypeStruct((2, groups // 2 * room), jnp.float32)
     return pl.pallas_call(
         filter_kernel,
         out_shape=(
             jax.ShapeDtypeStruct((rows, cells), jnp.bfloat16),
-            jax.ShapeDtypeStruct((2, cells), jnp.float32),
+            part,
+            part,
         ),
         in_specs=[vmem] * 4,
-        out_specs=(vmem, vmem),
-        scratch_shapes=[field, half, field, field, field],
+        out_specs=(vmem, vmem, vmem),
+        scratch_shapes=[pltpu.VMEM((2, cells), jnp.float32), field, half, field, field, field],
         compiler_params=pltpu.CompilerParams(vmem_limit_bytes=16 * 2**20),
         name="filter_box",
     )(marks, plain, near_diagonal, far)
 
 
-def by_halves(part, span):
-    half = part.shape[1] // 2
-    is_low = (lax.axis_index("grp") & span) == 0
-    low, high = part[:, :half], part[:, half:]
-    return jnp.where(is_low, low, high), jnp.where(is_low, high, low)
-
-
-def sum_blocks(halves):
+def sum_blocks(kept, sent, width):
     groups, devs = lax.axis_size("grp"), lax.axis_size("dev")
-    onward = [(d, (d + 1) % devs) for d in range(devs)]
-    if groups & (groups - 1) or groups == 1:
-        sums = lax.psum_scatter(halves, "grp", scatter_dimension=1, tiled=True)
-        return sums[:1] + lax.ppermute(sums[1:], "dev", onward)
     span = groups // 2
     while span > 1:
-        mine, other = by_halves(halves, span)
-        halves = mine + lax.ppermute(other, "grp", [(g, g ^ span) for g in range(groups)])
+        part = kept + lax.ppermute(sent, "grp", [(g, g ^ span) for g in range(groups)])
+        half = part.shape[1] // 2
+        kept, sent = part[:, :half], part[:, half:]
         span //= 2
-    mine, other = by_halves(halves, 1)
     both_axes = ("grp", "dev")
     places = [(g, d) for g in range(groups) for d in range(devs)]
-    carried = lax.ppermute(mine[1:], both_axes, [(g * devs + d, g * devs + (d + 1) % devs) for g, d in places])
-    beside = lax.ppermute(other[:1], both_axes, [(g * devs + d, (g ^ 1) * devs + d) for g, d in places])
-    slanted = lax.ppermute(other[1:], both_axes, [(g * devs + d, (g ^ 1) * devs + (d + 1) % devs) for g, d in places])
-    return mine[:1] + carried + slanted + beside
+    carried = lax.ppermute(kept[1:], both_axes, [(g * devs + d, g * devs + (d + 1) % devs) for g, d in places])
+    beside = lax.ppermute(sent[:1], both_axes, [(g * devs + d, (g ^ 1) * devs + d) for g, d in places])
+    slanted = lax.ppermute(sent[1:], both_axes, [(g * devs + d, (g ^ 1) * devs + (d + 1) % devs) for g, d in places])
+    return (kept[:1] + beside + carried + slanted)[:, :width]
 
 
 def on_device(orbitals, potential, counts, parity):
@@ -271,8 +282,8 @@
     marks = jnp.concatenate([counts, parity], 1)
     eye = make_eye()
     plain, near_diagonal = turn_orbitals(orbitals[0, 0], potential, eye)
-    filtered_rows, halves = filter_box(marks, plain, near_diagonal, far)
-    density = sum_blocks(halves)
+    filtered_rows, kept, sent = filter_box(marks, plain, near_diagonal, far)
+    density = sum_blocks(kept, sent, cells // lax.axis_size("grp"))
     filtered = jnp.swapaxes(filtered_rows.reshape(2, slots, cells), 0, 1)
     return density[None], filtered[None, None]
 

time: 19.8 us -> 19.1 us (0.965)
  waiting for transfers between devices: 4.48 us -> 3.8 us
    ppermute x4, waiting for transfers between devices: 4.46 us -> 3.77 us  [the longest x1 1.98 us: sum_blocks(): lax.ppermute(sent, 'grp', [(g, g ^ span) for g in range(groups)])]
where the time goes in v7:
time: 19.1 us; the launch traced here: 19 us
  starting transfers between devices  7.76 us (41%)
  Pallas kernels  3.97 us (21%)
  waiting for transfers between devices  3.8 us (20%)
  local copies, waits for them, and re-layouts  1.44 us (8%)
  between operations  1.34 us (7%)
  other arithmetic  0.67 us (4%)
    ppermute x1, starting transfers between devices, on_device(): lax.ppermute(potential, 'dev', [((i + 1) % group_size, i) for i in range(...  3.39 us
    pallas_call x1, Pallas kernels, filter_box(): pl.pallas_call(filter_kernel, out_shape=(jax.ShapeDtypeStruct((rows, cell...  3.16 us
    ppermute x1, starting transfers between devices, sum_blocks(): lax.ppermute(sent, 'grp', [(g, g ^ span) for g in range(groups)])  2.61 us
    ppermute x1, waiting for transfers between devices, sum_blocks(): lax.ppermute(sent, 'grp', [(g, g ^ span) for g in range(groups)])  1.98 us
    ppermute x1, waiting for transfers between devices, sum_blocks(): lax.ppermute(sent[1:], both_axes, [(g * devs + d, (g ^ 1) * devs + (d + 1...  1.67 us
    reshape x1, local copies, waits for them, and re-layouts, on_device(): filtered = jnp.swapaxes(filtered_rows.reshape(2, slots, cells), 0, 1)  1.42 us
    ppermute x1, starting transfers between devices, sum_blocks(): lax.ppermute(kept[1:], both_axes, [(g * devs + d, g * devs + (d + 1) % de...  0.98 us
    pallas_call x1, Pallas kernels, turn_orbitals(): pl.pallas_call(turn_kernel, out_shape=(jax.ShapeDtypeStruct((cells, plane...  0.8 us
  transfers between devices with their start and end apart: 5, of which 3 were waited for; matrix products, arithmetic and copies ran while one was open for 8% of the time, Pallas kernels for 4%

profile of v7, /device:TPU:0, one launch (start us, length us, event | category | flops | bytes accessed | tf_op | source)
XLA Modules:
  0.0 19.0 jit_solution(15601708623443812925)
XLA Ops:
  0.6 0.0 copy-start.1
  0.6 0.0 copy-start.2
  0.6 0.0 copy-start
  0.7 3.4 %collective-permute-start = (bf16[1,2304]{1,0:T(2,128)(2,1)}, bf16[1,2304]{1,0:T(2,128)(2,1)S(1)}, u32[]{:S(2)}, u32[]{:S(2)}) collective-permute-start(bf16[1,2304]{1,0:T(2,128)(2,1)} %near_ref.1), channel_id=1, source_target_pairs={{1,0},{2,1},{3,2},{4,3},{5,4},{6,5},{7,6},{0,7},{9,8},{10,9},{11,1... | collective-permute-start | bytes 13832 | tf_op jit(solution)/shard_map/ppermute | solution.py:281
  4.7 0.0 copy-done.2
  4.7 0.1 pad_add_fusion.marks_ref
  4.8 0.0 copy-done.1
  4.8 0.0 copy-done
  4.8 0.8 %turn_orbitals.1 = (f32[2304,128]{1,0:T(8,128)S(1)}, f32[1152,128]{1,0:T(8,128)S(1)}) custom-call(bf16[64,2,2304]{2,1,0:T(2,128)(2,1)S(1)} %bitcast.9, bf16[1,2304]{1,0:T(2,128)(2,1)S(1)} %copy-done.1, bf16[128,128]{1,0:T(8,128)(2,1)S(1)} %make_eye.1.eye_ref), custom_call_target="tpu_custom_call" | custom-call | tf_op jit(solution)/shard_map/turn_orbitals/pallas_call | solution.py:227
  5.6 0.0 collective-permute-done.far_ref
  5.6 3.2 %filter_box.1 = (bf16[128,2304]{1,0:T(8,128)(2,1)S(1)}, f32[2,1280]{1,0:T(2,128)S(1)}, f32[2,1280]{1,0:T(2,128)S(1)}) custom-call(s32[1,9]{1,0:T(1,128)S(1)} %pad_add_fusion.marks_ref, f32[2304,128]{1,0:T(8,128)S(1)} %get-tuple-element.7.plain, f32[1152,128]{1,0:T(8,128)S(1)} %get-tuple-element.8.near_diagonal, bf16[1,2304]{1,0:T(2,128)(2,1)S(1)} %collective-permute-done.far_ref), custom_call_target="tpu_custom_call" | custom-call | tf_op jit(solution)/shard_map/filter_box/pallas_call | solution.py:247
  8.8 2.6 %collective-permute-start.1 = (f32[2,1280]{1,0:T(2,128)S(1)}, f32[2,1280]{1,0:T(2,128)S(1)}, u32[]{:S(2)}, u32[]{:S(2)}) collective-permute-start(f32[2,1280]{1,0:T(2,128)S(1)} %get-tuple-element.10), channel_id=1, source_target_pairs={{0,16},{8,24},{16,0},{24,8},{1,17},{9,25},{17,1},{25,9},{2,18},{10... | collective-permute-start | bytes 30728 | tf_op jit(solution)/shard_map/ppermute | solution.py:266
  11.4 2.0 %collective-permute-done.1 = f32[2,1280]{1,0:T(2,128)S(1)} collective-permute-done((f32[2,1280]{1,0:T(2,128)S(1)}, f32[2,1280]{1,0:T(2,128)S(1)}, u32[]{:S(2)}, u32[]{:S(2)}) %collective-permute-start.1) | collective-permute-done | bytes 10272 | tf_op jit(solution)/shard_map/ppermute | solution.py:266
  13.4 0.1 collective-permute-start.4
  13.5 1.0 %collective-permute-start.3 = (f32[1,640]{1,0:T(1,128)S(1)}, f32[1,640]{1,0:T(1,128)S(1)}, u32[]{:S(2)}, u32[]{:S(2)}) collective-permute-start(f32[1,640]{1,0:T(1,128)S(1)} %get-tuple-element.14), channel_id=1, source_target_pairs={{0,1},{1,2},{2,3},{3,4},{4,5},{5,6},{6,7},{7,0},{8,9},{9,10},{10,1... | collective-permute-start | bytes 7688 | tf_op jit(solution)/shard_map/ppermute | solution.py:272
  14.4 0.7 %collective-permute-start.2 = (f32[1,640]{1,0:T(1,128)S(1)}, f32[1,640]{1,0:T(1,128)S(1)}, u32[]{:S(2)}, u32[]{:S(2)}) collective-permute-start(f32[1,640]{1,0:T(1,128)S(1)} %get-tuple-element.15), channel_id=1, source_target_pairs={{0,8},{1,9},{2,10},{3,11},{4,12},{5,13},{6,14},{7,15},{8,0},{9,1},... | collective-permute-start | bytes 7688 | tf_op jit(solution)/shard_map/ppermute | solution.py:273
  15.2 1.4 %copy.8 = bf16[2,64,2304]{2,0,1:T(2,128)(2,1)} copy(bf16[2,64,2304]{2,1,0:T(8,128)(2,1)S(1)} %bitcast.10) | data formatting | bytes 1179648 | tf_op jit(solution)/shard_map/reshape | solution.py:287
  16.6 1.7 %collective-permute-done.4 = f32[1,640]{1,0:T(1,128)S(1)} collective-permute-done((f32[1,640]{1,0:T(1,128)S(1)}, f32[1,640]{1,0:T(1,128)S(1)}, u32[]{:S(2)}, u32[]{:S(2)}) %collective-permute-start.4) | collective-permute-done | bytes 2592 | tf_op jit(solution)/shard_map/ppermute | solution.py:274
  18.3 0.1 collective-permute-done.3
  18.4 0.0 collective-permute-done.2
  18.4 0.6 %fusion = f32[1,1,576]{2,1,0:T(1,128)} fusion(f32[1,640]{1,0:T(1,128)S(1)} %collective-permute-done.4, f32[1,640]{1,0:T(1,128)S(1)} %collective-permute-done.3, f32[1,640]{1,0:T(1,128)S(1)} %collective-permute-done.2, f32[1,640]{1,0:T(1,128)S(1)} %get-tuple-element.12), kind=kLoop, calls=%fused_computation.2 | loop fusion | flops 1728 | bytes 11520 | tf_op jit(solution)/shard_map/broadcast_in_dim | solution.py:288
  (3 shorter events, 0.0 us)
Async XLA Ops:
  0.6 4.2 %copy-start.1 = (bf16[1,2304]{1,0:T(2,128)(2,1)S(1)}, bf16[1,2304]{1,0:T(2,128)(2,1)}, u32[]{:S(2)}) copy-start(bf16[1,2304]{1,0:T(2,128)(2,1)} %near_ref.1) | copy-start | bytes 13828
  0.6 4.1 %copy-start.2 = (s32[1,8]{1,0:T(1,128)S(1)}, s32[1,8]{1,0:T(1,128)}, u32[]{:S(2)}) copy-start(s32[1,8]{1,0:T(1,128)} %param.6) | copy-start | bytes 100
  0.6 4.2 %copy-start = (bf16[1,1,64,2,2304]{4,3,2,1,0:T(2,128)(2,1)S(1)}, bf16[1,1,64,2,2304]{4,3,2,1,0:T(2,128)(2,1)}, u32[]{:S(2)}) copy-start(bf16[1,1,64,2,2304]{4,3,2,1,0:T(2,128)(2,1)} %param.4) | copy-start | bytes 1769476
  0.7 5.0 %collective-permute-start = (bf16[1,2304]{1,0:T(2,128)(2,1)}, bf16[1,2304]{1,0:T(2,128)(2,1)S(1)}, u32[]{:S(2)}, u32[]{:S(2)}) collective-permute-start(bf16[1,2304]{1,0:T(2,128)(2,1)} %near_ref.1), channel_id=1, source_target_pairs={{1,0},{2,1},{3,2},{4,3},{5,4},{6,5},{7,6},{0,7},{9,8},{10,9},{11,1... | collective-permute-start | bytes 13832 | tf_op jit(solution)/shard_map/ppermute | solution.py:281
  8.8 4.6 %collective-permute-start.1 = (f32[2,1280]{1,0:T(2,128)S(1)}, f32[2,1280]{1,0:T(2,128)S(1)}, u32[]{:S(2)}, u32[]{:S(2)}) collective-permute-start(f32[2,1280]{1,0:T(2,128)S(1)} %get-tuple-element.10), channel_id=1, source_target_pairs={{0,16},{8,24},{16,0},{24,8},{1,17},{9,25},{17,1},{25,9},{2,18},{10... | collective-permute-start | bytes 30728 | tf_op jit(solution)/shard_map/ppermute | solution.py:266
  13.4 4.9 %collective-permute-start.4 = (f32[1,640]{1,0:T(1,128)S(1)}, f32[1,640]{1,0:T(1,128)S(1)}, u32[]{:S(2)}, u32[]{:S(2)}) collective-permute-start(f32[1,640]{1,0:T(1,128)S(1)} %get-tuple-element.13), channel_id=1, source_target_pairs={{0,9},{1,10},{2,11},{3,12},{4,13},{5,14},{6,15},{7,8},{8,1},{9,2},... | collective-permute-start | bytes 7688 | tf_op jit(solution)/shard_map/ppermute | solution.py:274
  13.5 4.9 %collective-permute-start.3 = (f32[1,640]{1,0:T(1,128)S(1)}, f32[1,640]{1,0:T(1,128)S(1)}, u32[]{:S(2)}, u32[]{:S(2)}) collective-permute-start(f32[1,640]{1,0:T(1,128)S(1)} %get-tuple-element.14), channel_id=1, source_target_pairs={{0,1},{1,2},{2,3},{3,4},{4,5},{5,6},{6,7},{7,0},{8,9},{9,10},{10,1... | collective-permute-start | bytes 7688 | tf_op jit(solution)/shard_map/ppermute | solution.py:272
  14.4 3.9 %collective-permute-start.2 = (f32[1,640]{1,0:T(1,128)S(1)}, f32[1,640]{1,0:T(1,128)S(1)}, u32[]{:S(2)}, u32[]{:S(2)}) collective-permute-start(f32[1,640]{1,0:T(1,128)S(1)} %get-tuple-element.15), channel_id=1, source_target_pairs={{0,8},{1,9},{2,10},{3,11},{4,12},{5,13},{6,14},{7,15},{8,0},{9,1},... | collective-permute-start | bytes 7688 | tf_op jit(solution)/shard_map/ppermute | solution.py:273

commit v8 on v7

--- a/solution.py
+++ b/solution.py
@@ -197,17 +197,18 @@
     me = lax.axis_index("grp")
     width = cells // groups
     room = kept_ref.shape[1] // (groups // 2)
-    parts = [halves_ref[:, i * width : (i + 1) * width] for i in range(groups)]
+    padding = jnp.zeros((2, room - width), jnp.float32)
+    parts = [
+        jnp.concatenate([halves_ref[:, i * width : (i + 1) * width], padding], 1) for i in range(groups)
+    ]
     span = 1
     while span < groups:
         swapped = (me & span) != 0
         parts = [jnp.where(swapped, parts[j ^ span], parts[j]) for j in range(groups)]
         span *= 2
-    kept_ref[...] = jnp.zeros(kept_ref.shape, jnp.float32)
-    sent_ref[...] = jnp.zeros(sent_ref.shape, jnp.float32)
     for j in range(groups // 2):
-        kept_ref[:, j * room : j * room + width] = parts[j]
-        sent_ref[:, j * room : j * room + width] = parts[groups // 2 + j]
+        kept_ref[:, j * room : (j + 1) * room] = parts[j]
+        sent_ref[:, j * room : (j + 1) * room] = parts[groups // 2 + j]
 
 
 def make_eye():

time: 19.1 us -> 19.1 us (level)
  no operation moved by 1% of the time
where the time goes in v8:
time: 19.1 us; the launch traced here: 19 us
  starting transfers between devices  7.81 us (41%)
  Pallas kernels  3.9 us (20%)
  waiting for transfers between devices  3.8 us (20%)
  local copies, waits for them, and re-layouts  1.44 us (8%)
  between operations  1.35 us (7%)
  other arithmetic  0.67 us (4%)
    ppermute x1, starting transfers between devices, on_device(): lax.ppermute(potential, 'dev', [((i + 1) % group_size, i) for i in range(...  3.39 us
    pallas_call x1, Pallas kernels, filter_box(): pl.pallas_call(filter_kernel, out_shape=(jax.ShapeDtypeStruct((rows, cell...  3.09 us
    ppermute x1, starting transfers between devices, sum_blocks(): lax.ppermute(sent, 'grp', [(g, g ^ span) for g in range(groups)])  2.66 us
    ppermute x1, waiting for transfers between devices, sum_blocks(): lax.ppermute(sent, 'grp', [(g, g ^ span) for g in range(groups)])  1.98 us
    ppermute x1, waiting for transfers between devices, sum_blocks(): lax.ppermute(sent[1:], both_axes, [(g * devs + d, (g ^ 1) * devs + (d + 1...  1.67 us
    reshape x1, local copies, waits for them, and re-layouts, on_device(): filtered = jnp.swapaxes(filtered_rows.reshape(2, slots, cells), 0, 1)  1.42 us
    ppermute x1, starting transfers between devices, sum_blocks(): lax.ppermute(kept[1:], both_axes, [(g * devs + d, g * devs + (d + 1) % de...  0.98 us
    pallas_call x1, Pallas kernels, turn_orbitals(): pl.pallas_call(turn_kernel, out_shape=(jax.ShapeDtypeStruct((cells, plane...  0.8 us
  transfers between devices with their start and end apart: 5, of which 3 were waited for; matrix products, arithmetic and copies ran while one was open for 8% of the time, Pallas kernels for 4%

profile of v8, /device:TPU:0, one launch (start us, length us, event | category | flops | bytes accessed | tf_op | source)
XLA Modules:
  0.0 19.0 jit_solution(6245797909782200374)
XLA Ops:
  0.6 0.0 copy-start.1
  0.6 0.0 copy-start.2
  0.6 0.0 copy-start
  0.7 3.4 %collective-permute-start = (bf16[1,2304]{1,0:T(2,128)(2,1)}, bf16[1,2304]{1,0:T(2,128)(2,1)S(1)}, u32[]{:S(2)}, u32[]{:S(2)}) collective-permute-start(bf16[1,2304]{1,0:T(2,128)(2,1)} %near_ref.1), channel_id=1, source_target_pairs={{1,0},{2,1},{3,2},{4,3},{5,4},{6,5},{7,6},{0,7},{9,8},{10,9},{11,1... | collective-permute-start | bytes 13832 | tf_op jit(solution)/shard_map/ppermute | solution.py:282
  4.7 0.0 copy-done.2
  4.7 0.1 pad_add_fusion.marks_ref
  4.8 0.0 copy-done.1
  4.8 0.0 copy-done
  4.8 0.8 %turn_orbitals.1 = (f32[2304,128]{1,0:T(8,128)S(1)}, f32[1152,128]{1,0:T(8,128)S(1)}) custom-call(bf16[64,2,2304]{2,1,0:T(2,128)(2,1)S(1)} %bitcast.9, bf16[1,2304]{1,0:T(2,128)(2,1)S(1)} %copy-done.1, bf16[128,128]{1,0:T(8,128)(2,1)S(1)} %make_eye.1.eye_ref), custom_call_target="tpu_custom_call" | custom-call | tf_op jit(solution)/shard_map/turn_orbitals/pallas_call | solution.py:228
  5.6 0.0 collective-permute-done.far_ref
  5.6 3.1 %filter_box.1 = (bf16[128,2304]{1,0:T(8,128)(2,1)S(1)}, f32[2,1280]{1,0:T(2,128)S(1)}, f32[2,1280]{1,0:T(2,128)S(1)}) custom-call(s32[1,9]{1,0:T(1,128)S(1)} %pad_add_fusion.marks_ref, f32[2304,128]{1,0:T(8,128)S(1)} %get-tuple-element.7.plain, f32[1152,128]{1,0:T(8,128)S(1)} %get-tuple-element.8.near_diagonal, bf16[1,2304]{1,0:T(2,128)(2,1)S(1)} %collective-permute-done.far_ref), custom_call_target="tpu_custom_call" | custom-call | tf_op jit(solution)/shard_map/filter_box/pallas_call | solution.py:248
  8.7 2.7 %collective-permute-start.1 = (f32[2,1280]{1,0:T(2,128)S(1)}, f32[2,1280]{1,0:T(2,128)S(1)}, u32[]{:S(2)}, u32[]{:S(2)}) collective-permute-start(f32[2,1280]{1,0:T(2,128)S(1)} %get-tuple-element.10), channel_id=1, source_target_pairs={{0,16},{8,24},{16,0},{24,8},{1,17},{9,25},{17,1},{25,9},{2,18},{10... | collective-permute-start | bytes 30728 | tf_op jit(solution)/shard_map/ppermute | solution.py:267
  11.4 2.0 %collective-permute-done.1 = f32[2,1280]{1,0:T(2,128)S(1)} collective-permute-done((f32[2,1280]{1,0:T(2,128)S(1)}, f32[2,1280]{1,0:T(2,128)S(1)}, u32[]{:S(2)}, u32[]{:S(2)}) %collective-permute-start.1) | collective-permute-done | bytes 10272 | tf_op jit(solution)/shard_map/ppermute | solution.py:267
  13.4 0.1 collective-permute-start.4
  13.5 1.0 %collective-permute-start.3 = (f32[1,640]{1,0:T(1,128)S(1)}, f32[1,640]{1,0:T(1,128)S(1)}, u32[]{:S(2)}, u32[]{:S(2)}) collective-permute-start(f32[1,640]{1,0:T(1,128)S(1)} %get-tuple-element.14), channel_id=1, source_target_pairs={{0,1},{1,2},{2,3},{3,4},{4,5},{5,6},{6,7},{7,0},{8,9},{9,10},{10,1... | collective-permute-start | bytes 7688 | tf_op jit(solution)/shard_map/ppermute | solution.py:273
  14.4 0.7 %collective-permute-start.2 = (f32[1,640]{1,0:T(1,128)S(1)}, f32[1,640]{1,0:T(1,128)S(1)}, u32[]{:S(2)}, u32[]{:S(2)}) collective-permute-start(f32[1,640]{1,0:T(1,128)S(1)} %get-tuple-element.15), channel_id=1, source_target_pairs={{0,8},{1,9},{2,10},{3,11},{4,12},{5,13},{6,14},{7,15},{8,0},{9,1},... | collective-permute-start | bytes 7688 | tf_op jit(solution)/shard_map/ppermute | solution.py:274
  15.2 1.4 %copy.8 = bf16[2,64,2304]{2,0,1:T(2,128)(2,1)} copy(bf16[2,64,2304]{2,1,0:T(8,128)(2,1)S(1)} %bitcast.10) | data formatting | bytes 1179648 | tf_op jit(solution)/shard_map/reshape | solution.py:288
  16.6 1.7 %collective-permute-done.4 = f32[1,640]{1,0:T(1,128)S(1)} collective-permute-done((f32[1,640]{1,0:T(1,128)S(1)}, f32[1,640]{1,0:T(1,128)S(1)}, u32[]{:S(2)}, u32[]{:S(2)}) %collective-permute-start.4) | collective-permute-done | bytes 2592 | tf_op jit(solution)/shard_map/ppermute | solution.py:275
  18.3 0.1 collective-permute-done.3
  18.4 0.0 collective-permute-done.2
  18.4 0.6 %fusion = f32[1,1,576]{2,1,0:T(1,128)} fusion(f32[1,640]{1,0:T(1,128)S(1)} %collective-permute-done.4, f32[1,640]{1,0:T(1,128)S(1)} %collective-permute-done.3, f32[1,640]{1,0:T(1,128)S(1)} %collective-permute-done.2, f32[1,640]{1,0:T(1,128)S(1)} %get-tuple-element.12), kind=kLoop, calls=%fused_computation.2 | loop fusion | flops 1728 | bytes 11520 | tf_op jit(solution)/shard_map/broadcast_in_dim | solution.py:289
  (3 shorter events, 0.0 us)
Async XLA Ops:
  0.6 4.2 %copy-start.1 = (bf16[1,2304]{1,0:T(2,128)(2,1)S(1)}, bf16[1,2304]{1,0:T(2,128)(2,1)}, u32[]{:S(2)}) copy-start(bf16[1,2304]{1,0:T(2,128)(2,1)} %near_ref.1) | copy-start | bytes 13828
  0.6 4.1 %copy-start.2 = (s32[1,8]{1,0:T(1,128)S(1)}, s32[1,8]{1,0:T(1,128)}, u32[]{:S(2)}) copy-start(s32[1,8]{1,0:T(1,128)} %param.6) | copy-start | bytes 100
  0.6 4.2 %copy-start = (bf16[1,1,64,2,2304]{4,3,2,1,0:T(2,128)(2,1)S(1)}, bf16[1,1,64,2,2304]{4,3,2,1,0:T(2,128)(2,1)}, u32[]{:S(2)}) copy-start(bf16[1,1,64,2,2304]{4,3,2,1,0:T(2,128)(2,1)} %param.4) | copy-start | bytes 1769476
  0.7 5.0 %collective-permute-start = (bf16[1,2304]{1,0:T(2,128)(2,1)}, bf16[1,2304]{1,0:T(2,128)(2,1)S(1)}, u32[]{:S(2)}, u32[]{:S(2)}) collective-permute-start(bf16[1,2304]{1,0:T(2,128)(2,1)} %near_ref.1), channel_id=1, source_target_pairs={{1,0},{2,1},{3,2},{4,3},{5,4},{6,5},{7,6},{0,7},{9,8},{10,9},{11,1... | collective-permute-start | bytes 13832 | tf_op jit(solution)/shard_map/ppermute | solution.py:282
  8.7 4.6 %collective-permute-start.1 = (f32[2,1280]{1,0:T(2,128)S(1)}, f32[2,1280]{1,0:T(2,128)S(1)}, u32[]{:S(2)}, u32[]{:S(2)}) collective-permute-start(f32[2,1280]{1,0:T(2,128)S(1)} %get-tuple-element.10), channel_id=1, source_target_pairs={{0,16},{8,24},{16,0},{24,8},{1,17},{9,25},{17,1},{25,9},{2,18},{10... | collective-permute-start | bytes 30728 | tf_op jit(solution)/shard_map/ppermute | solution.py:267
  13.4 4.9 %collective-permute-start.4 = (f32[1,640]{1,0:T(1,128)S(1)}, f32[1,640]{1,0:T(1,128)S(1)}, u32[]{:S(2)}, u32[]{:S(2)}) collective-permute-start(f32[1,640]{1,0:T(1,128)S(1)} %get-tuple-element.13), channel_id=1, source_target_pairs={{0,9},{1,10},{2,11},{3,12},{4,13},{5,14},{6,15},{7,8},{8,1},{9,2},... | collective-permute-start | bytes 7688 | tf_op jit(solution)/shard_map/ppermute | solution.py:275
  13.5 4.9 %collective-permute-start.3 = (f32[1,640]{1,0:T(1,128)S(1)}, f32[1,640]{1,0:T(1,128)S(1)}, u32[]{:S(2)}, u32[]{:S(2)}) collective-permute-start(f32[1,640]{1,0:T(1,128)S(1)} %get-tuple-element.14), channel_id=1, source_target_pairs={{0,1},{1,2},{2,3},{3,4},{4,5},{5,6},{6,7},{7,0},{8,9},{9,10},{10,1... | collective-permute-start | bytes 7688 | tf_op jit(solution)/shard_map/ppermute | solution.py:273
  14.4 3.9 %collective-permute-start.2 = (f32[1,640]{1,0:T(1,128)S(1)}, f32[1,640]{1,0:T(1,128)S(1)}, u32[]{:S(2)}, u32[]{:S(2)}) collective-permute-start(f32[1,640]{1,0:T(1,128)S(1)} %get-tuple-element.15), channel_id=1, source_target_pairs={{0,8},{1,9},{2,10},{3,11},{4,12},{5,13},{6,14},{7,15},{8,0},{9,1},... | collective-permute-start | bytes 7688 | tf_op jit(solution)/shard_map/ppermute | solution.py:274
